TPU v7x, 128 devices: a whole 4x4x4 slice. The times are simulated.
128 devices in a mesh: vol: 16 (over x, y), zone: 8 (over z, core).
Axes of the slice: x: 4, y: 4, z: 4, core: 2. Of those that a mesh axis runs over, the one named last changes fastest.
Arguments:
- load: float32 [3, 2048, 2048], P(None, 'vol', 'zone'), may hold values from -12 to 12
- support_stiffness: float32 [2048, 2048], P('vol', 'zone'), may hold values from 0.5 to 4
- plastic_flags: int32 [2048, 16], P('vol', 'zone'), may hold values 0 or 1
- owner_map: int32 [16, 8, 16], P('vol', 'zone'), may hold values from 0 to 7, as said below
- pattern: int32 [16, 8, 16, 3], P('vol', 'zone'), may hold values from 0 to 31, as said below
- active: int32 [16, 8, 16], P('vol', 'zone'), may hold values 0 or 1
- mortar: float32 [16, 8, 16, 3, 128, 128], P('vol', 'zone'), may hold values from -1 to 2
Outputs:
- displacement: float32 [3, 2048, 2048], P(None, 'vol', 'zone')
- residual: float32 [3, 2048, 2048], P(None, 'vol', 'zone')
Inputs may be any that keep to these rules, and one draw needn't show every extreme that they name: owner_map[i, s, m] is the zone index of the owner, in vol group i, of surface block m of device (i, s). At most 4 blocks of one device go to one owner, and in each vol group some owner receives exactly 4 blocks from every device. pattern[i, z, r] names slots of owner z of vol group i, slot s * 4 + k being the k-th block (in increasing block index) that device s of the group sends to z. Every entry names a slot that holds a block, unless the owner receives none (then all are 0), and every slot that holds a block is named.
All inputs are finite; a program needn't handle non-finite values. No bound on the sum of `plastic_flags` or of `active` on one device may be relied on, other than what follows from the above.
Results may differ from a plain program's by a relative error of at most 0.005.
Values sent between devices are 32-bit elements; how exact they have to be, the bound alone decides.
A program may use at most 64 MiB of HBM per device.

v0:
```python
import jax
import jax.numpy as jnp
from jax import lax
from jax.sharding import PartitionSpec as P

SROWS = 8
BLK = 128
KRY = 3
NEWTON = 2


yield_scale = 0.5
penalty = 2.0
plastic_hardening = 0.2


def extended(cells, sides, width):
    for axis, dim in sides:
        count = lax.axis_size(axis)
        ends = count - 1
        head = lax.slice_in_dim(cells, 0, width, axis=dim)
        tail = lax.slice_in_dim(cells, cells.shape[dim] - width, cells.shape[dim], axis=dim)
        cells = jnp.concatenate(
            [
                lax.ppermute(tail, axis, [(i, (i + 1) % count) for i in range(ends)]),
                cells,
                lax.ppermute(head, axis, [((i + 1) % count, i) for i in range(ends)]),
            ],
            axis=dim,
        )
    return cells


def grid_part(grid_values):
    padded = extended(grid_values, (("vol", 1), ("zone", 2)), 1)
    beside = padded[:, 2:, 1:-1] + padded[:, :-2, 1:-1] + padded[:, 1:-1, 2:] + padded[:, 1:-1, :-2]
    return 4.0 * grid_values - beside


def block_ranks(owners):
    number = owners.shape[-1]
    matching = owners[..., :, None] == owners[..., None, :]
    earlier = jnp.arange(number)[:, None] < jnp.arange(number)[None, :]
    return jnp.sum((matching & earlier).astype(jnp.int32), axis=-2)


def mortar_forces(slot_values, slot_links, switches, couplings):
    orient = jnp.where(jnp.arange(slot_links.shape[1]) == 0, 1.0, -1.0).astype(jnp.float32)
    picked = slot_values[slot_links] * orient[None, :, None, None]
    gap_values = jnp.einsum("rkij,rkcj->rci", couplings, picked, precision=lax.Precision.HIGHEST)
    multipliers = penalty * switches.astype(jnp.float32)[:, None, None] * gap_values
    pushed = jnp.einsum("rkij,rci->rkcj", couplings, multipliers, precision=lax.Precision.HIGHEST)
    pushed = pushed * orient[None, :, None, None]
    flattened = pushed.reshape(-1, pushed.shape[2], pushed.shape[3])
    return jax.ops.segment_sum(flattened, slot_links.reshape(-1), num_segments=slot_values.shape[0])


def surface_of(grid_values):
    surface_rows = grid_values[:, :SROWS, :]
    column_blocks = surface_rows.shape[2] // BLK
    shaped = surface_rows.reshape(3, SROWS, column_blocks, BLK).transpose(1, 2, 0, 3)
    return shaped.reshape(SROWS * column_blocks, 3, BLK)


def field_of(blocks, height, breadth):
    column_blocks = breadth // BLK
    shaped = (
        blocks.reshape(SROWS, column_blocks, 3, BLK)
        .transpose(2, 0, 1, 3)
        .reshape(3, SROWS, breadth)
    )
    return jnp.pad(shaped, ((0, 0), (0, height - SROWS), (0, 0)))


def squared_total(remainder):
    return lax.psum(jnp.sum(remainder * remainder), ("vol", "zone"))


def local(load, support_stiffness, plastic_flags, owner_map, pattern, active, mortar):
    zone_count = lax.axis_size("zone")
    owners = owner_map[0, 0]
    number = owners.shape[0]
    capacity = 2 * number // zone_count
    slot_count = zone_count * capacity
    slot_links = pattern[0, 0]
    switches = active[0, 0]
    couplings = mortar[0, 0]
    height, breadth = (load.shape[1], load.shape[2])
    hardness = jnp.where(plastic_flags == 1, plastic_hardening, 1.0).astype(jnp.float32)
    hardness = jnp.broadcast_to(hardness[:, :, None], (height, breadth // BLK, BLK)).reshape(
        height, breadth
    )
    slot_ids = jnp.arange(slot_count, dtype=jnp.int32)
    every_owner = lax.all_gather(owner_map, "zone", axis=1, tiled=True)[0, 0:zone_count]
    block_order = block_ranks(every_owner)
    target = jnp.arange(zone_count, dtype=jnp.int32)[:, None] * capacity + block_order
    owned_here = every_owner == lax.axis_index("zone")
    picker = (
        owned_here.reshape(-1)[None, :] & (target.reshape(-1)[None, :] == slot_ids[:, None])
    ).astype(jnp.float32)

    def contact(grid_values):
        blocks = surface_of(grid_values)
        gathered = lax.all_gather(blocks[None], "zone", axis=0, tiled=True)
        slot_values = jnp.einsum(
            "sq,qcb->scb", picker, gathered.reshape(-1, 3, BLK), precision=lax.Precision.HIGHEST
        )
        forces = mortar_forces(slot_values, slot_links, switches, couplings)
        spread = jnp.einsum("sq,scb->qcb", picker, forces, precision=lax.Precision.HIGHEST)
        summed = lax.psum_scatter(
            spread.reshape(zone_count, number, 3, BLK), "zone", scatter_dimension=0, tiled=True
        )
        return field_of(summed[0], height, breadth)

    def residual_of(moved):
        material = support_stiffness * (
            hardness * moved + (1.0 - hardness) * yield_scale * jnp.tanh(moved / yield_scale)
        )
        return grid_part(moved) + material + contact(moved) - load

    displacement = jnp.zeros_like(load)
    for newton_step in range(NEWTON):
        saturation = jnp.tanh(displacement / yield_scale)
        onsite = support_stiffness * (hardness + (1.0 - hardness) * (1.0 - saturation * saturation))
        update = jnp.zeros_like(load)
        remainder = -residual_of(displacement)
        direction = remainder
        norm_now = squared_total(remainder)
        for krylov_step in range(KRY):
            applied = grid_part(direction) + onsite * direction + contact(direction)
            step_length = norm_now / lax.psum(jnp.sum(direction * applied), ("vol", "zone"))
            update = update + step_length * direction
            remainder = remainder - step_length * applied
            norm_next = squared_total(remainder)
            direction = remainder + norm_next / norm_now * direction
            norm_now = norm_next
        displacement = displacement + update
    return (displacement, residual_of(displacement))


def solution(mesh):
    in_specs = (
        P(None, "vol", "zone"),
        P("vol", "zone"),
        P("vol", "zone"),
        P("vol", "zone", None),
        P("vol", "zone", None, None),
        P("vol", "zone", None),
        P("vol", "zone", None, None, None, None),
    )
    out_specs = (P(None, "vol", "zone"), P(None, "vol", "zone"))
    return jax.shard_map(local, mesh=mesh, in_specs=in_specs, out_specs=out_specs, check_vma=False)
```

profile of v0, /device:TPU:1, one launch (start us, length us, event | category | flops | bytes accessed | tf_op | source)
XLA Modules:
  0.0 1614.7 jit_solution(1832730383167304781)
XLA Ops:
  48.4 49.2 %all-reduce.32.cloned.1.call-done = f32[8,16,3,128]{3,1,0,2:T(8,128)} async-done(((f32[8,16,3,128]{3,1,0,2:T(8,128)}), f32[8,16,3,128]{3,1,0,2:T(8,128)}) %all-reduce.32.cloned.1.call-update) | async-done | bytes 196624
  104.3 15.9 all_gather.29
  151.7 52.0 %all-reduce.34.cloned.1.call-done = f32[8,16,3,128]{3,1,0,2:T(8,128)} async-done(((f32[8,16,3,128]{3,1,0,2:T(8,128)}), f32[8,16,3,128]{3,1,0,2:T(8,128)}) %all-reduce.34.cloned.1.call-update) | async-done | bytes 196624
  209.9 67.1 %all-reduce.21 = (f32[]{:T(128)}, f32[]{:T(128)}) all-reduce(f32[]{:T(128)} %get-tuple-element.5, f32[]{:T(128)} %get-tuple-element.4), channel_id=1, replica_groups=mesh['vol'=16,'zone'=8] {'vol','zone'}, use_global_device_ids=true, to_apply=%region_4.5 | all-reduce | flops 2 | bytes 16 | tf_op jit(solution)/shard_map/psum | solution.py:76
  282.0 62.6 %psum.86 = f32[]{:T(128)} all-reduce(f32[]{:T(128)} %get-tuple-element.19), channel_id=1, replica_groups=mesh['vol'=16,'zone'=8] {'vol','zone'}, use_global_device_ids=true, to_apply=%region_10.11 | all-reduce | flops 1 | bytes 8 | tf_op jit(solution)/shard_map/psum | solution.py:76
  393.0 49.7 %all-reduce.36.cloned.1.call-done = f32[8,16,3,128]{3,1,0,2:T(8,128)} async-done(((f32[8,16,3,128]{3,1,0,2:T(8,128)}), f32[8,16,3,128]{3,1,0,2:T(8,128)}) %all-reduce.36.cloned.1.call-update) | async-done | bytes 196624
  448.9 67.0 %psum.87 = f32[]{:T(128)} all-reduce(f32[]{:T(128)} %get-tuple-element.17), channel_id=1, replica_groups=mesh['vol'=16,'zone'=8] {'vol','zone'}, use_global_device_ids=true, to_apply=%region_14.15 | all-reduce | flops 1 | bytes 8 | tf_op jit(solution)/shard_map/psum | solution.py:131
  519.0 62.7 %psum.88 = f32[]{:T(128)} all-reduce(f32[]{:T(128)} %multiply_reduce_fusion.5), channel_id=1, replica_groups=mesh['vol'=16,'zone'=8] {'vol','zone'}, use_global_device_ids=true, to_apply=%region_16.17 | all-reduce | flops 1 | bytes 8 | tf_op jit(solution)/shard_map/psum | solution.py:76
  590.6 13.9 all_gather.31
  627.0 49.8 %all-reduce.38.cloned.1.call-done = f32[8,16,3,128]{3,1,0,2:T(8,128)} async-done(((f32[8,16,3,128]{3,1,0,2:T(8,128)}), f32[8,16,3,128]{3,1,0,2:T(8,128)}) %all-reduce.38.cloned.1.call-update) | async-done | bytes 196624
  683.8 67.0 %psum.89 = f32[]{:T(128)} all-reduce(f32[]{:T(128)} %fusion.190), channel_id=1, replica_groups=mesh['vol'=16,'zone'=8] {'vol','zone'}, use_global_device_ids=true, to_apply=%region_20.21 | all-reduce | flops 1 | bytes 8 | tf_op jit(solution)/shard_map/psum | solution.py:131
  799.3 49.7 %all-reduce.40.cloned.1.call-done = f32[8,16,3,128]{3,1,0,2:T(8,128)} async-done(((f32[8,16,3,128]{3,1,0,2:T(8,128)}), f32[8,16,3,128]{3,1,0,2:T(8,128)}) %all-reduce.40.cloned.1.call-update) | async-done | bytes 196624
  856.0 15.9 all_gather.33
  903.3 52.0 %all-reduce.42.cloned.1.call-done = f32[8,16,3,128]{3,1,0,2:T(8,128)} async-done(((f32[8,16,3,128]{3,1,0,2:T(8,128)}), f32[8,16,3,128]{3,1,0,2:T(8,128)}) %all-reduce.42.cloned.1.call-update) | async-done | bytes 196624
  962.6 67.1 %all-reduce.20 = (f32[]{:T(128)}, f32[]{:T(128)}) all-reduce(f32[]{:T(128)} %get-tuple-element.3, f32[]{:T(128)} %get-tuple-element.2), channel_id=1, replica_groups=mesh['vol'=16,'zone'=8] {'vol','zone'}, use_global_device_ids=true, to_apply=%region_24.25 | all-reduce | flops 2 | bytes 16 | tf_op jit(solution)/shard_map/psum | solution.py:76
  1033.4 62.6 %psum.92 = f32[]{:T(128)} all-reduce(f32[]{:T(128)} %get-tuple-element.12), channel_id=1, replica_groups=mesh['vol'=16,'zone'=8] {'vol','zone'}, use_global_device_ids=true, to_apply=%region_30.31 | all-reduce | flops 1 | bytes 8 | tf_op jit(solution)/shard_map/psum | solution.py:76
  1145.5 49.3 %all-reduce.44.cloned.1.call-done = f32[8,16,3,128]{3,1,0,2:T(8,128)} async-done(((f32[8,16,3,128]{3,1,0,2:T(8,128)}), f32[8,16,3,128]{3,1,0,2:T(8,128)}) %all-reduce.44.cloned.1.call-update) | async-done | bytes 196624
  1201.7 67.0 %psum.93 = f32[]{:T(128)} all-reduce(f32[]{:T(128)} %get-tuple-element.10), channel_id=1, replica_groups=mesh['vol'=16,'zone'=8] {'vol','zone'}, use_global_device_ids=true, to_apply=%region_34.35 | all-reduce | flops 1 | bytes 8 | tf_op jit(solution)/shard_map/psum | solution.py:131
  1271.9 62.7 %psum.94 = f32[]{:T(128)} all-reduce(f32[]{:T(128)} %multiply_reduce_fusion), channel_id=1, replica_groups=mesh['vol'=16,'zone'=8] {'vol','zone'}, use_global_device_ids=true, to_apply=%region_36.37 | all-reduce | flops 1 | bytes 8 | tf_op jit(solution)/shard_map/psum | solution.py:76
  1343.7 13.9 all_gather.35
  1383.4 49.5 %all-reduce.46.cloned.1.call-done = f32[8,16,3,128]{3,1,0,2:T(8,128)} async-done(((f32[8,16,3,128]{3,1,0,2:T(8,128)}), f32[8,16,3,128]{3,1,0,2:T(8,128)}) %all-reduce.46.cloned.1.call-update) | async-done | bytes 196624
  1439.2 67.0 %psum.95 = f32[]{:T(128)} all-reduce(f32[]{:T(128)} %fusion.163), channel_id=1, replica_groups=mesh['vol'=16,'zone'=8] {'vol','zone'}, use_global_device_ids=true, to_apply=%region_40.41 | all-reduce | flops 1 | bytes 8 | tf_op jit(solution)/shard_map/psum | solution.py:131
  1515.7 14.4 all_gather.36
  1552.4 48.9 %all-reduce.48.cloned.1.call-done = f32[8,16,3,128]{3,1,0,2:T(8,128)} async-done(((f32[8,16,3,128]{3,1,0,2:T(8,128)}), f32[8,16,3,128]{3,1,0,2:T(8,128)}) %all-reduce.48.cloned.1.call-update) | async-done | bytes 196624
  (321 shorter events, 410.2 us)
Async XLA Ops:
  7.2 90.5 %all-reduce.32.cloned.1.call-start = ((), (), s32[]{:S(2)}) async-start(), calls=%async_computation | async-start | bytes 393216
  39.5 164.1 %all-reduce.34.cloned.1.call-start = ((), (), s32[]{:S(2)}) async-start(), calls=%async_computation.1 | async-start | bytes 393216
  43.4 57.4 %collective-permute-start.3 = (f32[3,130,1]{2,1,0:T(8,128)}, f32[3,130,1]{2,1,0:T(8,128)}, u32[]{:S(2)}, u32[]{:S(2)}) collective-permute-start(f32[3,130,1]{2,1,0:T(8,128)} %get-tuple-element.40), channel_id=1, source_target_pairs={{0,1},{1,2},{2,3},{3,4},{4,5},{5,6},{6,7},{8,9},{9,10},{10,11},{11... | collective-permute-start | bytes 4688 | tf_op jit(solution)/shard_map/ppermute | solution.py:25
  45.4 55.5 %collective-permute-start.2 = (f32[3,130,1]{2,1,0:T(8,128)}, f32[3,130,1]{2,1,0:T(8,128)}, u32[]{:S(2)}, u32[]{:S(2)}) collective-permute-start(f32[3,130,1]{2,1,0:T(8,128)} %get-tuple-element.39), channel_id=1, source_target_pairs={{1,0},{2,1},{3,2},{4,3},{5,4},{6,5},{7,6},{9,8},{10,9},{11,10},{12... | collective-permute-start | bytes 4688 | tf_op jit(solution)/shard_map/ppermute | solution.py:27
  144.7 298.0 %all-reduce.36.cloned.1.call-start = ((), (), s32[]{:S(2)}) async-start(), calls=%async_computation.2 | async-start | bytes 393216
  146.7 60.2 %collective-permute-start.7 = (f32[3,130,1]{2,1,0:T(8,128)}, f32[3,130,1]{2,1,0:T(8,128)}, u32[]{:S(2)}, u32[]{:S(2)}) collective-permute-start(f32[3,130,1]{2,1,0:T(8,128)} %get-tuple-element.38), channel_id=1, source_target_pairs={{0,1},{1,2},{2,3},{3,4},{4,5},{5,6},{6,7},{8,9},{9,10},{10,11},{11... | collective-permute-start | bytes 4688 | tf_op jit(solution)/shard_map/ppermute | solution.py:25
  148.6 58.3 %collective-permute-start.6 = (f32[3,130,1]{2,1,0:T(8,128)}, f32[3,130,1]{2,1,0:T(8,128)}, u32[]{:S(2)}, u32[]{:S(2)}) collective-permute-start(f32[3,130,1]{2,1,0:T(8,128)} %get-tuple-element.37), channel_id=1, source_target_pairs={{1,0},{2,1},{3,2},{4,3},{5,4},{6,5},{7,6},{9,8},{10,9},{11,10},{12... | collective-permute-start | bytes 4688 | tf_op jit(solution)/shard_map/ppermute | solution.py:27
  385.5 291.3 %all-reduce.38.cloned.1.call-start = ((), (), s32[]{:S(2)}) async-start(), calls=%async_computation.3 | async-start | bytes 393216
  387.1 58.8 %collective-permute-start.11 = (f32[3,130,1]{2,1,0:T(8,128)}, f32[3,130,1]{2,1,0:T(8,128)}, u32[]{:S(2)}, u32[]{:S(2)}) collective-permute-start(f32[3,130,1]{2,1,0:T(8,128)} %get-tuple-element.36), channel_id=1, source_target_pairs={{0,1},{1,2},{2,3},{3,4},{4,5},{5,6},{6,7},{8,9},{9,10},{10,11},{11... | collective-permute-start | bytes 4688 | tf_op jit(solution)/shard_map/ppermute | solution.py:25
  620.2 228.7 %all-reduce.40.cloned.1.call-start = ((), (), s32[]{:S(2)}) async-start(), calls=%async_computation.4 | async-start | bytes 393216
  621.8 58.2 %collective-permute-start.15 = (f32[3,130,1]{2,1,0:T(8,128)}, f32[3,130,1]{2,1,0:T(8,128)}, u32[]{:S(2)}, u32[]{:S(2)}) collective-permute-start(f32[3,130,1]{2,1,0:T(8,128)} %get-tuple-element.34), channel_id=1, source_target_pairs={{0,1},{1,2},{2,3},{3,4},{4,5},{5,6},{6,7},{8,9},{9,10},{10,11},{11... | collective-permute-start | bytes 4688 | tf_op jit(solution)/shard_map/ppermute | solution.py:25
  625.1 55.0 %collective-permute-start.14 = (f32[3,130,1]{2,1,0:T(8,128)}, f32[3,130,1]{2,1,0:T(8,128)}, u32[]{:S(2)}, u32[]{:S(2)}) collective-permute-start(f32[3,130,1]{2,1,0:T(8,128)} %get-tuple-element.33), channel_id=1, source_target_pairs={{1,0},{2,1},{3,2},{4,3},{5,4},{6,5},{7,6},{9,8},{10,9},{11,10},{12... | collective-permute-start | bytes 4688 | tf_op jit(solution)/shard_map/ppermute | solution.py:27
  792.7 162.6 %all-reduce.42.cloned.1.call-start = ((), (), s32[]{:S(2)}) async-start(), calls=%async_computation.5 | async-start | bytes 393216
  794.3 57.9 %collective-permute-start.19 = (f32[3,130,1]{2,1,0:T(8,128)}, f32[3,130,1]{2,1,0:T(8,128)}, u32[]{:S(2)}, u32[]{:S(2)}) collective-permute-start(f32[3,130,1]{2,1,0:T(8,128)} %get-tuple-element.32), channel_id=1, source_target_pairs={{0,1},{1,2},{2,3},{3,4},{4,5},{5,6},{6,7},{8,9},{9,10},{10,11},{11... | collective-permute-start | bytes 4688 | tf_op jit(solution)/shard_map/ppermute | solution.py:25
  796.2 56.0 %collective-permute-start.18 = (f32[3,130,1]{2,1,0:T(8,128)}, f32[3,130,1]{2,1,0:T(8,128)}, u32[]{:S(2)}, u32[]{:S(2)}) collective-permute-start(f32[3,130,1]{2,1,0:T(8,128)} %get-tuple-element.31), channel_id=1, source_target_pairs={{1,0},{2,1},{3,2},{4,3},{5,4},{6,5},{7,6},{9,8},{10,9},{11,10},{12... | collective-permute-start | bytes 4688 | tf_op jit(solution)/shard_map/ppermute | solution.py:27
  896.3 298.5 %all-reduce.44.cloned.1.call-start = ((), (), s32[]{:S(2)}) async-start(), calls=%async_computation.6 | async-start | bytes 393216
  898.3 60.3 %collective-permute-start.23 = (f32[3,130,1]{2,1,0:T(8,128)}, f32[3,130,1]{2,1,0:T(8,128)}, u32[]{:S(2)}, u32[]{:S(2)}) collective-permute-start(f32[3,130,1]{2,1,0:T(8,128)} %get-tuple-element.30), channel_id=1, source_target_pairs={{0,1},{1,2},{2,3},{3,4},{4,5},{5,6},{6,7},{8,9},{9,10},{10,11},{11... | collective-permute-start | bytes 4688 | tf_op jit(solution)/shard_map/ppermute | solution.py:25
  900.2 58.4 %collective-permute-start.22 = (f32[3,130,1]{2,1,0:T(8,128)}, f32[3,130,1]{2,1,0:T(8,128)}, u32[]{:S(2)}, u32[]{:S(2)}) collective-permute-start(f32[3,130,1]{2,1,0:T(8,128)} %get-tuple-element.29), channel_id=1, source_target_pairs={{1,0},{2,1},{3,2},{4,3},{5,4},{6,5},{7,6},{9,8},{10,9},{11,10},{12... | collective-permute-start | bytes 4688 | tf_op jit(solution)/shard_map/ppermute | solution.py:27
  1137.7 295.2 %all-reduce.46.cloned.1.call-start = ((), (), s32[]{:S(2)}) async-start(), calls=%async_computation.7 | async-start | bytes 393216
  1139.6 58.4 %collective-permute-start.27 = (f32[3,130,1]{2,1,0:T(8,128)}, f32[3,130,1]{2,1,0:T(8,128)}, u32[]{:S(2)}, u32[]{:S(2)}) collective-permute-start(f32[3,130,1]{2,1,0:T(8,128)} %get-tuple-element.28), channel_id=1, source_target_pairs={{0,1},{1,2},{2,3},{3,4},{4,5},{5,6},{6,7},{8,9},{9,10},{10,11},{11... | collective-permute-start | bytes 4688 | tf_op jit(solution)/shard_map/ppermute | solution.py:25
  1376.3 225.0 %all-reduce.48.cloned.1.call-start = ((), (), s32[]{:S(2)}) async-start(), calls=%async_computation.8 | async-start | bytes 393216
  1378.2 57.9 %collective-permute-start.31 = (f32[3,130,1]{2,1,0:T(8,128)}, f32[3,130,1]{2,1,0:T(8,128)}, u32[]{:S(2)}, u32[]{:S(2)}) collective-permute-start(f32[3,130,1]{2,1,0:T(8,128)} %get-tuple-element.26), channel_id=1, source_target_pairs={{0,1},{1,2},{2,3},{3,4},{4,5},{5,6},{6,7},{8,9},{9,10},{10,11},{11... | collective-permute-start | bytes 4688 | tf_op jit(solution)/shard_map/ppermute | solution.py:25
  1547.5 57.1 %collective-permute-start.35 = (f32[3,130,1]{2,1,0:T(8,128)}, f32[3,130,1]{2,1,0:T(8,128)}, u32[]{:S(2)}, u32[]{:S(2)}) collective-permute-start(f32[3,130,1]{2,1,0:T(8,128)} %get-tuple-element.24), channel_id=1, source_target_pairs={{0,1},{1,2},{2,3},{3,4},{4,5},{5,6},{6,7},{8,9},{9,10},{10,11},{11... | collective-permute-start | bytes 4688 | tf_op jit(solution)/shard_map/ppermute | solution.py:25
  1549.4 55.2 %collective-permute-start.34 = (f32[3,130,1]{2,1,0:T(8,128)}, f32[3,130,1]{2,1,0:T(8,128)}, u32[]{:S(2)}, u32[]{:S(2)}) collective-permute-start(f32[3,130,1]{2,1,0:T(8,128)} %get-tuple-element.23), channel_id=1, source_target_pairs={{1,0},{2,1},{3,2},{4,3},{5,4},{6,5},{7,6},{9,8},{10,9},{11,10},{12... | collective-permute-start | bytes 4688 | tf_op jit(solution)/shard_map/ppermute | solution.py:27
  (43 other events, 1362.3 us)
Sparse Core Ops, SparseCore 0:
  39.6 57.9 all-reduce.31
  144.9 58.7 all-reduce.33
  385.6 57.0 all-reduce.35
  620.3 56.3 all-reduce.37
  792.8 56.0 all-reduce.39
  896.5 58.7 all-reduce.41
  1137.8 56.9 all-reduce.43
  1376.4 56.4 all-reduce.45
  1545.7 55.5 all-reduce.47
where the time goes:
time: 1630 us; the launch traced here: 1610 us
  blocking collectives  780 us (48%)
  waiting for transfers between devices  450 us (28%)
  other arithmetic  108 us (7%)
  starting transfers between devices  101 us (6%)
  matrix products  75.7 us (5%)
  local copies, waits for them, and re-layouts  72.1 us (4%)
  between operations  27.7 us (2%)
    unnamed x18, waiting for transfers between devices  450 us
    psum x6, blocking collectives, squared_total(): return lax.psum(jnp.sum(remainder * remainder), ('vol', 'zone'))  385 us
    psum x4, blocking collectives, local(): lax.psum(jnp.sum(direction * applied), ('vol', 'zone'))  268 us
    all_gather x8, blocking collectives, contact(): gathered = lax.all_gather(blocks[None], 'zone', axis=0, tiled=True)  115 us
    ppermute x18, starting transfers between devices, extended(): lax.ppermute(tail, axis, [(i, (i + 1) % count) for i in range(ends)])  65.6 us
    scatter-add x9, other arithmetic, mortar_forces(): jax.ops.segment_sum(flattened, slot_links.reshape(-1), num_segments=slot_...  46.9 us
    dot_general x9, matrix products, mortar_forces(): jnp.einsum('rkij,rkcj->rci', couplings, picked, precision=lax.Precision.H...  36.5 us
    ppermute x18, starting transfers between devices, extended(): lax.ppermute(head, axis, [((i + 1) % count, i) for i in range(ends)])  34.8 us
  transfers between devices with their start and end apart: 45, of which 9 were waited for; matrix products, arithmetic and copies ran while one was open for 9% of the time, Pallas kernels for 0%

commit v1 on v0

v1 whole, which is shorter than its diff:
```python
import functools

import jax
import jax.numpy as jnp
from jax import lax
from jax.experimental import pallas as pl
from jax.experimental.pallas import tpu as pltpu
from jax.sharding import PartitionSpec as P

SROWS = 8
BLK = 128
NNZ = 3
CAP = 4
KRY = 3
NEWTON = 2
STEPS = KRY * NEWTON
PAD = 8

yield_scale = 0.5
penalty = 2.0
plastic_hardening = 0.2

F32 = jnp.float32
BF16 = jnp.bfloat16


def kernel(
    n_vol, n_zone,
    load_ref, stiff_ref, flags_ref, owner_ref, pattern_ref, active_ref, mortar_ref,
    u_ref, res_ref,
    x_ref, p_ref, t_ref, l_ref, d_ref, lu_ref, hard_ref,
    mort_ref, mhi_ref, mlo_ref, spread_ref, push_ref,
    surf_ref, block_ref, back_ref,
    pack_tab, unpack_tab,
    fsend, frecv, bsend, brecv, rsend, rrecv, csend, crecv, zsend, zrecv, vsend, vrecv,
    msem, fs, fr, bs, br, rs, rr, cs, cr, zs, zr, vs, vr,
):
    comps, height = load_ref.shape[0], load_ref.shape[1]
    halves = load_ref.shape[2] // BLK
    groups = height // 8
    blocks = SROWS * halves
    rows = active_ref.shape[2]
    zone = lax.axis_index("zone")
    vol = lax.axis_index("vol")

    mortar_copy = pltpu.make_async_copy(mortar_ref.at[0, 0], mort_ref, msem)
    mortar_copy.start()

    def at_zone(step):
        return lax.rem(zone + step, n_zone)

    def at_vol(step):
        return lax.rem(vol + step, n_vol)

    barrier = pltpu.get_barrier_semaphore()
    for step in range(1, n_zone):
        pl.semaphore_signal(barrier, inc=1, device_id={"zone": at_zone(step)})
    for step in range(1, n_vol):
        pl.semaphore_signal(barrier, inc=1, device_id={"vol": at_vol(step)})

    owners = [owner_ref[0, 0, m] for m in range(blocks)]
    weights = []
    for m in range(blocks):
        weight, rank = jnp.int32(1), jnp.int32(0)
        for e in range(m):
            same = owners[e] == owners[m]
            weight = jnp.where(same, weight * 32, weight)
            rank = rank + jnp.where(same, 1, 0)
        weights.append(weight)
        unpack_tab[m] = owners[m] * CAP + rank
    for z in range(n_zone):
        code = jnp.int32(0)
        for m in range(blocks):
            code = code + jnp.where(owners[m] == z, weights[m] * (blocks + m), 0)
        for k in range(CAP):
            field = lax.shift_right_logical(code, 5 * k) & 31
            pack_tab[z * CAP + k] = jnp.where(field >= blocks, field - blocks, blocks)

    sub = lax.broadcasted_iota(jnp.int32, (8, BLK), 0)
    lane = lax.broadcasted_iota(jnp.int32, (8, BLK), 1)

    wide = rows * NNZ * 8
    link_lane = lax.broadcasted_iota(jnp.int32, (1, wide), 1)
    links = jnp.zeros((1, wide), jnp.int32)
    for r in range(rows):
        for k in range(NNZ):
            links = jnp.where(link_lane // 8 == r * NNZ + k, pattern_ref[0, 0, r, k], links)
    out_row = lax.broadcasted_iota(jnp.int32, (n_zone * CAP * 4, wide), 0)
    out_lane = lax.broadcasted_iota(jnp.int32, (n_zone * CAP * 4, wide), 1)
    hit = (out_row // 4 == links) & (lax.rem(out_row, 4) == lax.rem(out_lane, 4))
    spread_ref[...] = jnp.where(hit, 1.0, 0.0).astype(BF16)

    surf_ref[...] = jnp.zeros_like(surf_ref)
    block_ref[blocks] = jnp.zeros((8, BLK), F32)
    back_ref[...] = jnp.zeros_like(back_ref)
    rsend[...] = jnp.zeros_like(rsend)
    u_ref[...] = jnp.zeros_like(u_ref)
    lu_ref[...] = jnp.zeros_like(lu_ref)
    p_ref[...] = jnp.zeros_like(p_ref)
    t_ref[...] = jnp.zeros_like(t_ref)
    for c in range(comps):
        for b in range(halves):
            x_ref[c, b, 0:PAD, :] = jnp.zeros((PAD, BLK), F32)
            x_ref[c, b, PAD + height:, :] = jnp.zeros((PAD, BLK), F32)
            x_ref[c, b, PAD:PAD + height, :] = load_ref[c, :, b * BLK:(b + 1) * BLK]
            d_ref[c, b] = stiff_ref[:, b * BLK:(b + 1) * BLK]
    for b in range(halves):
        flag = jnp.broadcast_to(flags_ref[:, b:b + 1], (height, BLK))
        hard_ref[b] = jnp.where(flag == 1, plastic_hardening, 1.0).astype(F32)

    pl.semaphore_wait(barrier, n_zone - 1 + n_vol - 1)

    def remote(src, dst, send, recv, target):
        return pltpu.make_async_remote_copy(
            src_ref=src, dst_ref=dst, send_sem=send, recv_sem=recv, device_id=target
        )

    def await_bytes(ref, sem):
        pltpu.make_async_copy(ref, ref, sem).wait()

    def slots_of(z):
        return pl.ds(z * CAP, CAP)

    def group_rows(g):
        return pl.ds(pl.multiple_of(PAD + g * 8, 8), 8)

    def tile_rows(g):
        return pl.ds(pl.multiple_of(g * 8, 8), 8)

    def fold(total):
        return jnp.sum(total, axis=0, keepdims=True)

    def hardened(b, g):
        return stiff_ref[tile_rows(g), b * BLK:(b + 1) * BLK], hard_ref[b, tile_rows(g), :]

    def iteration(it, carry):
        gamma_old, step_old, pq_old, cross = carry
        first = lax.rem(it, KRY) == 0

        for c in range(comps):
            for b in range(halves):
                surf_ref[pl.ds(b * 8 + c, SROWS, stride=8 * halves), :] = x_ref[c, b, PAD:PAD + SROWS, :]

        for m in range(blocks):
            block_ref[m] = surf_ref[m * 8:m * 8 + 8, :]

        def packed(z, k):
            return block_ref[pack_tab[z * CAP + k]][0:4]

        for step in range(1, n_zone):
            z = at_zone(step)
            for k in range(CAP):
                fsend[it, step, k] = packed(z, k)
            remote(
                fsend.at[it, step], frecv.at[it, slots_of(zone)], fs.at[it], fr.at[it], {"zone": z}
            ).start()
        for k in range(CAP):
            frecv[it, zone * CAP + k] = packed(zone, k)

        for c in range(comps):
            for b in range(halves):
                j = c * halves + b
                rsend[it, 0, j:j + 1, :] = x_ref[c, b, PAD:PAD + 1, :]
                rsend[it, 1, j:j + 1, :] = x_ref[c, b, PAD + height - 1:PAD + height, :]
        remote(rsend.at[it, 0], rrecv.at[it, 1], rs.at[it], rr.at[it], {"vol": at_vol(n_vol - 1)}).start()
        remote(rsend.at[it, 1], rrecv.at[it, 0], rs.at[it], rr.at[it], {"vol": at_vol(1)}).start()
        for side, b, column in ((0, 0, 0), (1, halves - 1, BLK - 1)):
            strip = jnp.zeros((8, BLK), F32)
            for c in range(comps):
                for g in range(groups):
                    tile = x_ref[c, b, PAD + g * 8:PAD + g * 8 + 8, :]
                    strip = jnp.where(
                        lane == c * groups + g, jnp.broadcast_to(tile[:, column:column + 1], (8, BLK)), strip
                    )
            csend[it, side] = strip
        remote(csend.at[it, 0], crecv.at[it, 1], cs.at[it], cr.at[it], {"zone": at_zone(n_zone - 1)}).start()
        remote(csend.at[it, 1], crecv.at[it, 0], cs.at[it], cr.at[it], {"zone": at_zone(1)}).start()

        def inner(g, sums):
            gamma, delta = sums
            for c in range(comps):
                tiles = [x_ref[c, b, group_rows(g), :] for b in range(halves)]
                to_right = [pltpu.roll(tile, 1, axis=1) for tile in tiles]
                to_left = [pltpu.roll(tile, BLK - 1, axis=1) for tile in tiles]
                for b in range(halves):
                    x = tiles[b]
                    before = to_right[b - 1] if b > 0 else jnp.zeros_like(x)
                    after = to_left[b + 1] if b < halves - 1 else jnp.zeros_like(x)
                    left = jnp.where(lane == 0, before, to_right[b])
                    right = jnp.where(lane == BLK - 1, after, to_left[b])
                    over = x_ref[c, b, pl.ds(PAD + g * 8 - 1, 8), :]
                    under = x_ref[c, b, pl.ds(PAD + g * 8 + 1, 8), :]
                    image = 4.0 * x - (over + under + left + right)
                    l_ref[c, b, tile_rows(g), :] = image
                    gamma = gamma + x * x
                    delta = delta + x * (image + d_ref[c, b, tile_rows(g), :] * x)
            return gamma, delta

        zero = jnp.zeros((8, BLK), F32)
        gamma, delta = lax.fori_loop(0, groups, inner, (zero, zero), unroll=2)

        await_bytes(rrecv.at[it], rr.at[it])
        await_bytes(crecv.at[it], cr.at[it])
        over = jnp.where(vol == 0, 0.0, rrecv[it, 0])
        under = jnp.where(vol == n_vol - 1, 0.0, rrecv[it, 1])
        left = jnp.where(zone == 0, 0.0, crecv[it, 0])
        right = jnp.where(zone == n_zone - 1, 0.0, crecv[it, 1])
        delta = delta - (rsend[it, 0] * over + rsend[it, 1] * under)
        delta = delta - (csend[it, 0] * left + csend[it, 1] * right)

        @pl.when(it == 0)
        def _():
            mortar_copy.wait()

            def split(r, _):
                for k in range(NNZ):
                    piece = mort_ref[r, k] if k == 0 else -mort_ref[r, k]
                    high = piece.astype(BF16)
                    mhi_ref[r, :, k * BLK:(k + 1) * BLK] = high
                    mlo_ref[r, :, k * BLK:(k + 1) * BLK] = (piece - high.astype(F32)).astype(BF16)
                return 0

            lax.fori_loop(0, rows, split, 0)

        await_bytes(frecv.at[it, 0:(n_zone - 1) * CAP], fr.at[it])

        upper = lax.broadcasted_iota(jnp.int32, (8, NNZ * BLK), 0) < 4
        contract_last = (((1,), (1,)), ((), ()))

        def split_rows(both, mask):
            high = both.astype(BF16).astype(F32)
            return jnp.where(mask, high, both - high).astype(BF16)

        energy = zero
        pushes = []
        for r in range(rows):
            picked = jnp.concatenate([frecv[it, pattern_ref[0, 0, r, k]] for k in range(NNZ)], axis=1)
            picked = split_rows(jnp.concatenate([picked, picked], axis=0), upper)
            gap = lax.dot_general(picked, mhi_ref[r], contract_last, preferred_element_type=F32)
            gap = gap + lax.dot_general(picked, mlo_ref[r], contract_last, preferred_element_type=F32)
            gap = gap + pltpu.roll(gap, 4, axis=0)
            multiplier = (penalty * active_ref[0, 0, r].astype(F32)) * gap
            energy = energy + multiplier * gap
            pushes.append(multiplier)
        delta = delta + 0.5 * energy

        local = jnp.where(sub == 0, fold(gamma), jnp.where(sub == 1, fold(delta), fold(cross)))
        zsend[it] = local[0:4]
        zrecv[it, zone] = local[0:4]
        for step in range(1, n_zone):
            remote(zsend.at[it], zrecv.at[it, zone], zs.at[it], zr.at[it], {"zone": at_zone(step)}).start()

        for r in range(rows):
            multiplier = split_rows(pushes[r], sub < 4)
            force = jnp.dot(multiplier, mhi_ref[r], preferred_element_type=F32)
            force = force + jnp.dot(multiplier, mlo_ref[r], preferred_element_type=F32)
            force = force + pltpu.roll(force, 4, axis=0)
            high = force.astype(BF16).astype(F32)
            force = jnp.where(upper, high, force - high)
            for k in range(NNZ):
                at = (r * NNZ + k) * 8
                push_ref[at:at + 8, :] = force[:, k * BLK:(k + 1) * BLK]
        summed = jnp.dot(spread_ref[...], push_ref[...].astype(BF16), preferred_element_type=F32)
        bsend[it] = summed.reshape(n_zone * CAP, 4, BLK)
        for step in range(1, n_zone):
            z = at_zone(step)
            remote(
                bsend.at[it, slots_of(z)], brecv.at[it, slots_of(zone)], bs.at[it], br.at[it], {"zone": z}
            ).start()
        brecv[it, slots_of(zone)] = bsend[it, slots_of(zone)]

        for c in range(comps):
            for b in range(halves):
                j = c * halves + b
                l_ref[c, b, 0:1, :] = l_ref[c, b, 0:1, :] - over[j:j + 1]
                l_ref[c, b, height - 1:height, :] = l_ref[c, b, height - 1:height, :] - under[j:j + 1]
        for halo, b, column in ((left, 0, 0), (right, halves - 1, BLK - 1)):
            for c in range(comps):
                for g in range(groups):
                    j = c * groups + g
                    spread = jnp.broadcast_to(halo[:, j:j + 1], (8, BLK))
                    image = l_ref[c, b, g * 8:g * 8 + 8, :]
                    l_ref[c, b, g * 8:g * 8 + 8, :] = jnp.where(lane == column, image - spread, image)

        await_bytes(zrecv.at[it, 0:n_zone - 1], zr.at[it])
        part = jnp.sum(zrecv[it], axis=0)
        vsend[it] = part
        vrecv[it, vol] = part
        for step in range(1, n_vol):
            remote(vsend.at[it], vrecv.at[it, vol], vs.at[it], vr.at[it], {"vol": at_vol(step)}).start()

        await_bytes(brecv.at[it, 0:(n_zone - 1) * CAP], br.at[it])
        for m in range(blocks):
            back_ref[m * 8:m * 8 + 4, :] = brecv[it, unpack_tab[m]]
        for c in range(comps):
            for b in range(halves):
                contact = back_ref[pl.ds(b * 8 + c, SROWS, stride=8 * halves), :]
                l_ref[c, b, 0:SROWS, :] = l_ref[c, b, 0:SROWS, :] + contact

        await_bytes(vrecv.at[it, 0:n_vol - 1], vr.at[it])
        total = jnp.sum(jnp.sum(vrecv[it], axis=0), axis=1, keepdims=True)
        gamma, delta, cross = total[0:1], total[1:2], total[2:3]
        beta = jnp.where(first, 0.0, gamma / gamma_old)
        pq = delta + beta * (2.0 * cross + beta * pq_old)
        step_length = gamma / pq
        wide_beta = jnp.broadcast_to(beta, (8, BLK))
        wide_step = jnp.broadcast_to(step_length, (8, BLK))

        def update(g, cross):
            at = tile_rows(g)
            for c in range(comps):
                for b in range(halves):
                    x = x_ref[c, b, group_rows(g), :]
                    p = x + wide_beta * p_ref[c, b, at, :]
                    t = l_ref[c, b, at, :] + wide_beta * t_ref[c, b, at, :]
                    q = t + d_ref[c, b, at, :] * p
                    x = x - wide_step * q
                    p_ref[c, b, at, :] = p
                    t_ref[c, b, at, :] = t
                    x_ref[c, b, group_rows(g), :] = x
                    half = slice(b * BLK, (b + 1) * BLK)
                    u_ref[c, at, half] = u_ref[c, at, half] + wide_step * p
                    lu_ref[c, b, at, :] = lu_ref[c, b, at, :] + wide_step * t
                    cross = cross + x * q
            return cross

        cross = lax.fori_loop(0, groups, update, zero, unroll=2)

        @pl.when(lax.rem(it, KRY) == KRY - 1)
        def _():
            def newton(g, _):
                at = tile_rows(g)
                for b in range(halves):
                    stiff, hard = hardened(b, g)
                    half = slice(b * BLK, (b + 1) * BLK)
                    for c in range(comps):
                        u = u_ref[c, at, half]
                        bent = jnp.tanh(u / yield_scale)
                        material = stiff * (hard * u + (1.0 - hard) * yield_scale * bent)
                        residual = lu_ref[c, b, at, :] + material - load_ref[c, at, half]
                        res_ref[c, at, half] = residual
                        x_ref[c, b, group_rows(g), :] = -residual
                        d_ref[c, b, at, :] = stiff * (hard + (1.0 - hard) * (1.0 - bent * bent))
                return 0

            lax.fori_loop(0, groups, newton, 0)

        return gamma, step_length, pq, cross

    one = jnp.ones((1, 1), F32)
    lax.fori_loop(0, STEPS, iteration, (one, one, one, jnp.zeros((8, BLK), F32)))

    def drain(it, _):
        await_bytes(fsend.at[it, 0:n_zone - 1], fs.at[it])
        await_bytes(bsend.at[it, 0:(n_zone - 1) * CAP], bs.at[it])
        await_bytes(rsend.at[it], rs.at[it])
        await_bytes(csend.at[it], cs.at[it])
        await_bytes(zrecv.at[it, 0:n_zone - 1], zs.at[it])
        await_bytes(vrecv.at[it, 0:n_vol - 1], vs.at[it])
        return 0

    lax.fori_loop(0, STEPS, drain, 0)


def local(n_vol, n_zone, load, support_stiffness, plastic_flags, owner_map, pattern, active, mortar):
    comps, height, breadth = load.shape
    halves = breadth // BLK
    rows = active.shape[2]
    field = pltpu.VMEM((comps, halves, height, BLK), F32)
    slots = n_zone * CAP
    dma = pltpu.SemaphoreType.DMA
    vmem = pl.BlockSpec(memory_space=pltpu.VMEM)
    smem = pl.BlockSpec(memory_space=pltpu.SMEM)
    return pl.pallas_call(
        functools.partial(kernel, n_vol, n_zone),
        out_shape=[jax.ShapeDtypeStruct(load.shape, F32)] * 2,
        in_specs=[vmem, vmem, vmem, smem, smem, smem, pl.BlockSpec(memory_space=pl.ANY)],
        out_specs=[vmem, vmem],
        scratch_shapes=[
            pltpu.VMEM((comps, halves, height + 2 * PAD, BLK), F32),
            field, field, field, field, field,
            pltpu.VMEM((halves, height, BLK), F32),
            pltpu.VMEM(mortar.shape[2:], F32),
            pltpu.VMEM((rows, BLK, NNZ * BLK), BF16),
            pltpu.VMEM((rows, BLK, NNZ * BLK), BF16),
            pltpu.VMEM((slots * 4, rows * NNZ * 8), BF16),
            pltpu.VMEM((rows * NNZ * 8, BLK), F32),
            pltpu.VMEM((SROWS * halves * 8, BLK), F32),
            pltpu.VMEM((SROWS * halves + 1, 8, BLK), F32),
            pltpu.VMEM((SROWS * halves * 8, BLK), F32),
            pltpu.SMEM((slots,), jnp.int32),
            pltpu.SMEM((SROWS * halves,), jnp.int32),
            pltpu.VMEM((STEPS, n_zone, CAP, 4, BLK), F32),
            pltpu.VMEM((STEPS, slots, 4, BLK), F32),
            pltpu.VMEM((STEPS, slots, 4, BLK), F32),
            pltpu.VMEM((STEPS, slots, 4, BLK), F32),
            pltpu.VMEM((STEPS, 2, 8, BLK), F32),
            pltpu.VMEM((STEPS, 2, 8, BLK), F32),
            pltpu.VMEM((STEPS, 2, 8, BLK), F32),
            pltpu.VMEM((STEPS, 2, 8, BLK), F32),
            pltpu.VMEM((STEPS, 4, BLK), F32),
            pltpu.VMEM((STEPS, n_zone, 4, BLK), F32),
            pltpu.VMEM((STEPS, 4, BLK), F32),
            pltpu.VMEM((STEPS, n_vol, 4, BLK), F32),
            dma,
        ] + [dma((STEPS,))] * 12,
        compiler_params=pltpu.CompilerParams(
            collective_id=0, has_side_effects=True, vmem_limit_bytes=32 * 1024 * 1024
        ),
    )(load, support_stiffness, plastic_flags, owner_map, pattern, active, mortar)


def solution(mesh):
    in_specs = (
        P(None, "vol", "zone"),
        P("vol", "zone"),
        P("vol", "zone"),
        P("vol", "zone", None),
        P("vol", "zone", None, None),
        P("vol", "zone", None),
        P("vol", "zone", None, None, None, None),
    )
    out_specs = (P(None, "vol", "zone"), P(None, "vol", "zone"))
    body = functools.partial(local, mesh.shape["vol"], mesh.shape["zone"])
    return jax.shard_map(body, mesh=mesh, in_specs=in_specs, out_specs=out_specs, check_vma=False)
```

time: 1630 us -> 102 us (0.06)
  blocking collectives: 780 us -> 0 us
  waiting for transfers between devices: 450 us -> 0 us
  other arithmetic: 108 us -> 0 us
  starting transfers between devices: 101 us -> 0 us
  Pallas kernels: 0 us -> 93.4 us
  matrix products: 75.7 us -> 0 us
  local copies, waits for them, and re-layouts: 72.1 us -> 8.13 us
  between operations: 27.7 us -> 0.65 us
    psum x10 -> x0, blocking collectives: 653 us -> none  [the longest x6 385 us: squared_total(): return lax.psum(jnp.sum(remainder * remainder), ('vol', 'zone'))]
    unnamed x18 -> x0, waiting for transfers between devices: 450 us -> none
    all_gather x9 -> x0, blocking collectives: 128 us -> none  [the longest x8 115 us: contact(): gathered = lax.all_gather(blocks[None], 'zone', axis=0, tiled=True)]
    ppermute x36 -> x0, starting transfers between devices: 100 us -> none  [the longest x18 65.6 us: extended(): lax.ppermute(tail, axis, [(i, (i + 1) % count) for i in range(ends)])]
    pallas_call x0 -> x1, Pallas kernels: none -> 93.4 us  [local(): pl.pallas_call(functools.partial(kernel, n_vol, n_zone), out_shape=[jax.S...]
    dot_general x36 -> x0, matrix products: 75.7 us -> none  [the longest x9 36.5 us: mortar_forces(): jnp.einsum('rkij,rkcj->rci', couplings, picked, precision=lax.Precision.H...]
    scatter-add x9 -> x0, other arithmetic: 46.9 us -> none  [mortar_forces(): jax.ops.segment_sum(flattened, slot_links.reshape(-1), num_segments=slot_...]
    reduce_sum x11 -> x0, other arithmetic: 28.8 us -> none  [the longest x6 18.8 us: local(): jnp.sum(direction * applied)]
  transfers between devices with their start and end apart: 45 -> 0, of which waited for: 9 -> 0; matrix products, arithmetic and copies ran while one was open for 9% -> 0% of each run, Pallas kernels for 0% -> 0%
where the time goes in v1:
time: 102 us
  Pallas kernels  93.4 us (92%)
  local copies, waits for them, and re-layouts  8.13 us (8%)
    pallas_call x1, Pallas kernels, local(): pl.pallas_call(functools.partial(kernel, n_vol, n_zone), out_shape=[jax.S...  93.4 us
    unnamed x14, local copies, waits for them, and re-layouts  8.13 us

profile of v1, /device:TPU:1, one launch (start us, length us, event | category | flops | bytes accessed | tf_op | source)
XLA Modules:
  0.0 102.2 jit_solution(10694007167999848119)
XLA Ops:
  0.6 0.8 copy.10.pattern_ref
  1.4 0.8 copy.9.flags_ref
  2.2 0.0 copy-start
  2.2 1.9 %copy-done = f32[1,1,16,3,128,128]{5,4,3,2,1,0:T(8,128)S(1)} copy-done((f32[1,1,16,3,128,128]{5,4,3,2,1,0:T(8,128)S(1)}, f32[1,1,16,3,128,128]{5,4,3,2,1,0:T(8,128)}, u32[]{:S(2)}) %copy-start) | copy-done | bytes 3145752
  4.1 0.0 copy-start.1
  4.1 1.0 copy-done.1
  5.1 0.0 copy-start.2
  5.1 0.9 copy-done.2
  6.0 0.0 copy-start.3
  6.0 0.7 copy-done.3
  6.6 0.0 copy-start.4
  6.6 0.7 copy-done.4
  7.3 93.4 %shard_map.86 = (f32[3,128,256]{2,1,0:T(8,128)S(1)}, f32[3,128,256]{2,1,0:T(8,128)S(1)}) custom-call(f32[3,128,256]{2,1,0:T(8,128)S(1)} %copy-done.1, f32[128,256]{1,0:T(8,128)S(1)} %copy-done.2, s32[128,2]{1,0:T(8,128)S(1)} %copy.9.flags_ref, s32[1,1,16]{2,1,0:T(1,128)S(1)} %copy-done.3, s32[1,1,16,3]{3,2,1,0:T(8,128)S(1)} %copy.10.pattern_ref, ...), custom_call_target="tpu_custom_call" | custom-call | tf_op jit(solution)/shard_map/pallas_call | solution.py:374
  100.7 0.7 copy.13
  101.4 0.7 copy.14
Async XLA Ops:
  2.2 1.9 %copy-start = (f32[1,1,16,3,128,128]{5,4,3,2,1,0:T(8,128)S(1)}, f32[1,1,16,3,128,128]{5,4,3,2,1,0:T(8,128)}, u32[]{:S(2)}) copy-start(f32[1,1,16,3,128,128]{5,4,3,2,1,0:T(8,128)} %mortar_ref.1) | copy-start | bytes 9437188
  4.1 1.0 copy-start.1
  5.1 0.9 copy-start.2
  6.0 0.7 copy-start.3
  6.6 0.7 copy-start.4

commit v2 on v1

v2 whole, which is shorter than its diff:
```python
import functools

import jax
import jax.numpy as jnp
from jax import lax
from jax.experimental import pallas as pl
from jax.experimental.pallas import tpu as pltpu
from jax.sharding import PartitionSpec as P

SROWS = 8
BLK = 128
NNZ = 3
CAP = 4
KRY = 3
NEWTON = 2
STEPS = KRY * NEWTON
PAD = 8

yield_scale = 0.5
penalty = 2.0
plastic_hardening = 0.2

F32 = jnp.float32
BF16 = jnp.bfloat16


def kernel(
    n_vol, n_zone,
    load_hbm, stiff_hbm, flags_hbm, owner_hbm, pattern_hbm, active_hbm, mortar_ref,
    u_ref, res_ref,
    load_ref, stiff_ref, flags_ref, owner_ref, pattern_ref, active_ref, mort_ref,
    x_ref, l_ref, r_ref, d_ref, lu_ref, hard_ref, contact_ref, gap_ref, scale_ref,
    mhi_ref, mlo_ref, spread_ref, push_ref,
    surf_ref, block_ref, back_ref,
    pack_tab, unpack_tab,
    fsend, frecv, bsend, brecv, rsend, rrecv, csend, crecv, ssend, srecv,
    in_sem, fs, fr, bs, br, rs, rr, cs, cr, ss, sr,
):
    comps, height = load_ref.shape[0], load_ref.shape[1]
    halves = load_ref.shape[2] // BLK
    groups = height // 8
    blocks = SROWS * halves
    rows = active_ref.shape[2]
    devices = n_vol * n_zone
    zone = lax.axis_index("zone")
    vol = lax.axis_index("vol")

    inputs = [
        (owner_hbm, owner_ref), (pattern_hbm, pattern_ref), (active_hbm, active_ref), (flags_hbm, flags_ref),
        (load_hbm, load_ref), (stiff_hbm, stiff_ref), (mortar_ref.at[0, 0], mort_ref),
    ]
    fetches = [pltpu.make_async_copy(src, dst, in_sem.at[i]) for i, (src, dst) in enumerate(inputs)]
    for fetch in fetches:
        fetch.start()

    def at_zone(step):
        return lax.rem(zone + step, n_zone) if step else zone

    def at_vol(step):
        return lax.rem(vol + step, n_vol) if step else vol

    side = 4

    def hops(offset):
        around = [offset[0] // side, offset[0] % side, (offset[1] + 1) // 2]
        return sum(min(a % side, side - a % side) for a in around)

    others = [(v, z) for v in range(n_vol) for z in range(n_zone) if (v, z) != (0, 0)]
    others.sort(key=lambda offset: -hops(offset))

    barrier = pltpu.get_barrier_semaphore()
    for v, z in others:
        pl.semaphore_signal(barrier, inc=1, device_id={"vol": at_vol(v), "zone": at_zone(z)})

    sub = lax.broadcasted_iota(jnp.int32, (8, BLK), 0)
    lane = lax.broadcasted_iota(jnp.int32, (8, BLK), 1)
    zero = jnp.zeros((8, BLK), F32)

    for fetch in fetches[:4]:
        fetch.wait()
    owners = [owner_ref[0, 0, m] for m in range(blocks)]
    weights = []
    for m in range(blocks):
        weight, rank = jnp.int32(1), jnp.int32(0)
        for e in range(m):
            same = owners[e] == owners[m]
            weight = jnp.where(same, weight * 32, weight)
            rank = rank + jnp.where(same, 1, 0)
        weights.append(weight)
        unpack_tab[m] = owners[m] * CAP + rank
    for z in range(n_zone):
        code = jnp.int32(0)
        for m in range(blocks):
            code = code + jnp.where(owners[m] == z, weights[m] * (blocks + m), 0)
        for k in range(CAP):
            field = lax.shift_right_logical(code, 5 * k) & 31
            pack_tab[z * CAP + k] = jnp.where(field >= blocks, field - blocks, blocks)

    def link(r, k):
        return pattern_ref[0, k, 0, r]

    wide = rows * NNZ * 8
    link_lane = lax.broadcasted_iota(jnp.int32, (1, wide), 1)
    links = jnp.zeros((1, wide), jnp.int32)
    for r in range(rows):
        scale_ref[r * 8:r * 8 + 8, :] = jnp.full((8, BLK), penalty * active_ref[0, 0, r].astype(F32))
        for k in range(NNZ):
            links = jnp.where(link_lane // 8 == r * NNZ + k, link(r, k), links)
    out_row = lax.broadcasted_iota(jnp.int32, (n_zone * CAP * 4, wide), 0)
    out_lane = lax.broadcasted_iota(jnp.int32, (n_zone * CAP * 4, wide), 1)
    hit = (out_row // 4 == links) & (lax.rem(out_row, 4) == lax.rem(out_lane, 4))
    spread_ref[...] = jnp.where(hit, 1.0, 0.0).astype(BF16)

    surf_ref[...] = jnp.zeros_like(surf_ref)
    block_ref[blocks] = zero
    back_ref[...] = jnp.zeros_like(back_ref)
    rsend[...] = jnp.zeros_like(rsend)
    u_ref[...] = jnp.zeros_like(u_ref)
    lu_ref[...] = jnp.zeros_like(lu_ref)
    for b in range(halves):
        flag = jnp.transpose(jnp.broadcast_to(flags_ref[b:b + 1, :], (height, BLK)))
        hard_ref[b] = jnp.where(flag == 1, plastic_hardening, 1.0).astype(F32)
    for fetch in fetches[4:6]:
        fetch.wait()
    for c in range(comps):
        for b in range(halves):
            for j in range(KRY):
                x_ref[j, c, b, 0:PAD, :] = jnp.zeros((PAD, BLK), F32)
                x_ref[j, c, b, PAD + height:, :] = jnp.zeros((PAD, BLK), F32)
            x_ref[0, c, b, PAD:PAD + height, :] = load_ref[c, :, b * BLK:(b + 1) * BLK]
            d_ref[c, b] = stiff_ref[:, b * BLK:(b + 1) * BLK]
    fetches[6].wait()

    def split(r, _):
        for k in range(NNZ):
            piece = mort_ref[r, k] if k == 0 else -mort_ref[r, k]
            high = piece.astype(BF16)
            mhi_ref[r, :, k * BLK:(k + 1) * BLK] = high
            mlo_ref[r, :, k * BLK:(k + 1) * BLK] = (piece - high.astype(F32)).astype(BF16)
        return 0

    lax.fori_loop(0, rows, split, 0)

    pl.semaphore_wait(barrier, devices - 1)

    def remote(src, dst, send, recv, target):
        return pltpu.make_async_remote_copy(
            src_ref=src, dst_ref=dst, send_sem=send, recv_sem=recv, device_id=target
        )

    def await_bytes(ref, sem):
        pltpu.make_async_copy(ref, ref, sem).wait()

    def slots_of(z):
        return pl.ds(z * CAP, CAP)

    def group_rows(g):
        return pl.ds(pl.multiple_of(PAD + g * 8, 8), 8)

    def tile_rows(g):
        return pl.ds(pl.multiple_of(g * 8, 8), 8)

    def over_tiles(body, init):
        def group(g, carry):
            for c in range(comps):
                for b in range(halves):
                    carry = body(c, b, group_rows(g), tile_rows(g), carry)
            return carry

        return lax.fori_loop(0, groups, group, init, unroll=2)

    def send_field(j, it):
        for c in range(comps):
            for b in range(halves):
                surf_ref[pl.ds(b * 8 + c, SROWS, stride=8 * halves), :] = x_ref[j, c, b, PAD:PAD + SROWS, :]
        for m in range(blocks):
            block_ref[m] = surf_ref[m * 8:m * 8 + 8, :]
        for step in (4, 3, 5, 2, 6, 1, 7, 0):
            z = at_zone(step)
            for k in range(CAP):
                block = block_ref[pack_tab[z * CAP + k]][0:4]
                if step:
                    fsend[it, step, k] = block
                else:
                    frecv[it, zone * CAP + k] = block
            if step:
                remote(
                    fsend.at[it, step], frecv.at[it, slots_of(zone)], fs.at[it], fr.at[it], {"zone": z}
                ).start()
        for c in range(comps):
            for b in range(halves):
                i = c * halves + b
                rsend[it, 0, i:i + 1, :] = x_ref[j, c, b, PAD:PAD + 1, :]
                rsend[it, 1, i:i + 1, :] = x_ref[j, c, b, PAD + height - 1:PAD + height, :]
        remote(rsend.at[it, 0], rrecv.at[it, 1], rs.at[it], rr.at[it], {"vol": at_vol(n_vol - 1)}).start()
        remote(rsend.at[it, 1], rrecv.at[it, 0], rs.at[it], rr.at[it], {"vol": at_vol(1)}).start()
        for end, b, column in ((0, 0, 0), (1, halves - 1, BLK - 1)):
            strip = zero
            for c in range(comps):
                for g in range(groups):
                    tile = x_ref[j, c, b, PAD + g * 8:PAD + g * 8 + 8, :]
                    strip = jnp.where(
                        lane == c * groups + g, jnp.broadcast_to(tile[:, column:column + 1], (8, BLK)), strip
                    )
            csend[it, end] = strip
        remote(csend.at[it, 0], crecv.at[it, 1], cs.at[it], cr.at[it], {"zone": at_zone(n_zone - 1)}).start()
        remote(csend.at[it, 1], crecv.at[it, 0], cs.at[it], cr.at[it], {"zone": at_zone(1)}).start()

    def inner(j):
        def group(g, _):
            for c in range(comps):
                tiles = [x_ref[j, c, b, group_rows(g), :] for b in range(halves)]
                to_right = [pltpu.roll(tile, 1, axis=1) for tile in tiles]
                to_left = [pltpu.roll(tile, BLK - 1, axis=1) for tile in tiles]
                for b in range(halves):
                    before = to_right[b - 1] if b > 0 else zero
                    after = to_left[b + 1] if b < halves - 1 else zero
                    left = jnp.where(lane == 0, before, to_right[b])
                    right = jnp.where(lane == BLK - 1, after, to_left[b])
                    over = x_ref[j, c, b, pl.ds(PAD + g * 8 - 1, 8), :]
                    under = x_ref[j, c, b, pl.ds(PAD + g * 8 + 1, 8), :]
                    l_ref[j, c, b, tile_rows(g), :] = 4.0 * tiles[b] - (over + under + left + right)
            return 0

        lax.fori_loop(0, groups, group, 0, unroll=2)

    def outer(j, it):
        await_bytes(rrecv.at[it], rr.at[it])
        await_bytes(crecv.at[it], cr.at[it])
        over = jnp.where(vol == 0, 0.0, rrecv[it, 0])
        under = jnp.where(vol == n_vol - 1, 0.0, rrecv[it, 1])
        left = jnp.where(zone == 0, 0.0, crecv[it, 0])
        right = jnp.where(zone == n_zone - 1, 0.0, crecv[it, 1])
        for c in range(comps):
            for b in range(halves):
                i = c * halves + b
                l_ref[j, c, b, 0:1, :] = l_ref[j, c, b, 0:1, :] - over[i:i + 1]
                l_ref[j, c, b, height - 1:height, :] = l_ref[j, c, b, height - 1:height, :] - under[i:i + 1]
        for halo, b, column in ((left, 0, 0), (right, halves - 1, BLK - 1)):
            for c in range(comps):
                for g in range(groups):
                    i = c * groups + g
                    spread = jnp.broadcast_to(halo[:, i:i + 1], (8, BLK))
                    image = l_ref[j, c, b, g * 8:g * 8 + 8, :]
                    l_ref[j, c, b, g * 8:g * 8 + 8, :] = jnp.where(lane == column, image - spread, image)

    upper = lax.broadcasted_iota(jnp.int32, (8, NNZ * BLK), 0) < 4
    contract_last = (((1,), (1,)), ((), ()))

    def split_rows(both, mask):
        high = both.astype(BF16).astype(F32)
        return jnp.where(mask, high, both - high).astype(BF16)

    def find_gaps(j, it):
        await_bytes(frecv.at[it, 0:(n_zone - 1) * CAP], fr.at[it])
        for r in range(rows):
            picked = jnp.concatenate([frecv[it, link(r, k)] for k in range(NNZ)], axis=1)
            picked = split_rows(jnp.concatenate([picked, picked], axis=0), upper)
            gap = lax.dot_general(picked, mhi_ref[r], contract_last, preferred_element_type=F32)
            gap = gap + lax.dot_general(picked, mlo_ref[r], contract_last, preferred_element_type=F32)
            gap_ref[j, r * 8:r * 8 + 8, :] = gap + pltpu.roll(gap, 4, axis=0)

    def push_forces(j, it):
        for r in range(rows):
            at = slice(r * 8, r * 8 + 8)
            multiplier = split_rows(scale_ref[at, :] * gap_ref[j, at, :], sub < 4)
            force = jnp.dot(multiplier, mhi_ref[r], preferred_element_type=F32)
            force = force + jnp.dot(multiplier, mlo_ref[r], preferred_element_type=F32)
            force = force + pltpu.roll(force, 4, axis=0)
            high = force.astype(BF16).astype(F32)
            force = jnp.where(upper, high, force - high)
            for k in range(NNZ):
                to = (r * NNZ + k) * 8
                push_ref[to:to + 8, :] = force[:, k * BLK:(k + 1) * BLK]
        summed = jnp.dot(spread_ref[...], push_ref[...].astype(BF16), preferred_element_type=F32)
        bsend[it] = summed.reshape(n_zone * CAP, 4, BLK)
        for step in (4, 3, 5, 2, 6, 1, 7):
            z = at_zone(step)
            remote(
                bsend.at[it, slots_of(z)], brecv.at[it, slots_of(zone)], bs.at[it], br.at[it], {"zone": z}
            ).start()
        brecv[it, slots_of(zone)] = bsend[it, slots_of(zone)]

    def receive_forces(j, it):
        await_bytes(brecv.at[it, 0:(n_zone - 1) * CAP], br.at[it])
        for m in range(blocks):
            back_ref[m * 8:m * 8 + 4, :] = brecv[it, unpack_tab[m]]
        for c in range(comps):
            for b in range(halves):
                contact_ref[j, c, b] = back_ref[pl.ds(b * 8 + c, SROWS, stride=8 * halves), :]

    def energy(gaps):
        total = zero
        for r in range(rows):
            at = slice(r * 8, r * 8 + 8)
            gap = gaps(at)
            total = total + scale_ref[at, :] * (gap * gap)
        return 0.5 * total

    def start_sums(it, gamma, delta, cross):
        parts = []
        for part in (gamma, delta, cross):
            part = part + pltpu.roll(part, 64, axis=1)
            parts.append(part + pltpu.roll(part, 32, axis=1))
        mixed = jnp.where(lane < 32, parts[0], jnp.where(lane < 64, parts[1], parts[2]))
        mixed = jnp.sum(mixed, axis=0, keepdims=True)
        me = vol * n_zone + zone
        ssend[it] = mixed
        srecv[it, me] = mixed
        for v, z in others:
            target = {"vol": at_vol(v), "zone": at_zone(z)}
            remote(ssend.at[it], srecv.at[it, me], ss.at[it], sr.at[it], target).start()

    def finish_sums(it):
        await_bytes(srecv.at[it, 0:devices - 1], sr.at[it])
        total = jnp.sum(srecv[it], axis=0)
        place = lane[0:1]
        return [
            jnp.sum(jnp.where(place // 32 == i, total, 0.0), axis=1, keepdims=True) for i in range(3)
        ]

    def full(scalar):
        return jnp.broadcast_to(scalar, (8, BLK))

    def next_field(j):
        def tile(c, b, padded, at, _):
            x_ref[j + 1, c, b, padded, :] = l_ref[j, c, b, at, :] + d_ref[c, b, at, :] * x_ref[j, c, b, padded, :]
            return 0

        over_tiles(tile, 0)

    def add_contact(j):
        for c in range(comps):
            for b in range(halves):
                at = slice(PAD, PAD + SROWS)
                x_ref[j + 1, c, b, at, :] = x_ref[j + 1, c, b, at, :] + contact_ref[j, c, b]

    def newton(n, _):
        it = n * KRY

        send_field(0, it)
        inner(0)
        find_gaps(0, it)
        push_forces(0, it)
        outer(0, it)

        def dots0(c, b, padded, at, sums):
            x = x_ref[0, c, b, padded, :]
            q = l_ref[0, c, b, at, :] + d_ref[c, b, at, :] * x
            x_ref[1, c, b, padded, :] = q
            return sums[0] + x * x, sums[1] + x * q

        gamma, delta = over_tiles(dots0, (zero, zero))
        start_sums(it, gamma, delta + energy(lambda at: gap_ref[0, at, :]), zero)
        receive_forces(0, it)
        add_contact(0)

        send_field(1, it + 1)
        inner(1)
        gamma0, pq0, _ = finish_sums(it)
        a0 = gamma0 / pq0
        find_gaps(1, it + 1)
        push_forces(1, it + 1)
        outer(1, it + 1)
        w0 = full(a0)

        def dots1(c, b, padded, at, sums):
            x1 = x_ref[1, c, b, padded, :]
            r = x_ref[0, c, b, padded, :] - w0 * x1
            r_ref[c, b, at, :] = r
            q = (l_ref[0, c, b, at, :] - w0 * l_ref[1, c, b, at, :]) + d_ref[c, b, at, :] * r
            x_ref[2, c, b, padded, :] = l_ref[1, c, b, at, :] + d_ref[c, b, at, :] * x1
            return sums[0] + r * r, sums[1] + r * q, sums[2] + r * x1

        gamma, delta, cross = over_tiles(dots1, (zero, zero, zero))
        start_sums(it + 1, gamma, delta + energy(lambda at: gap_ref[0, at, :] - w0 * gap_ref[1, at, :]), cross)
        receive_forces(1, it + 1)
        add_contact(1)

        send_field(2, it + 2)
        inner(2)
        gamma1, delta, cross = finish_sums(it + 1)
        beta1 = gamma1 / gamma0
        pq1 = delta + beta1 * (2.0 * cross + beta1 * pq0)
        a1 = gamma1 / pq1
        find_gaps(2, it + 2)
        outer(2, it + 2)
        more, w1 = full(1.0 + beta1), full(a1)

        def second(x0, x1, x2):
            image = more * x1 - w0 * x2
            return image, (x0 - w0 * x1) - w1 * image

        def dots2(c, b, padded, at, sums):
            image = more * x_ref[1, c, b, padded, :] - w0 * x_ref[2, c, b, padded, :]
            r = r_ref[c, b, at, :] - w1 * image
            _, q = second(l_ref[0, c, b, at, :], l_ref[1, c, b, at, :], l_ref[2, c, b, at, :])
            q = q + d_ref[c, b, at, :] * r
            return sums[0] + r * r, sums[1] + r * q, sums[2] + r * image

        gamma, delta, cross = over_tiles(dots2, (zero, zero, zero))
        stored = energy(lambda at: second(gap_ref[0, at, :], gap_ref[1, at, :], gap_ref[2, at, :])[1])
        start_sums(it + 2, gamma, delta + stored, cross)
        push_forces(2, it + 2)
        receive_forces(2, it + 2)
        gamma2, delta, cross = finish_sums(it + 2)
        beta2 = gamma2 / gamma1
        pq2 = delta + beta2 * (2.0 * cross + beta2 * pq1)
        a2 = gamma2 / pq2
        turned = beta2 * (1.0 + beta1)
        k0 = full(a0 + a1 * (1.0 + beta1) + a2 * (1.0 + turned))
        k1 = full(-(a1 * a0 + a2 * (a0 + a1 * (1.0 + beta1) + beta2 * a0)))
        k2 = full(a2 * a1 * a0)

        def mix(fields):
            return k0 * fields(0) + k1 * fields(1) + k2 * fields(2)

        for c in range(comps):
            for b in range(halves):
                lu_ref[c, b, 0:SROWS, :] = lu_ref[c, b, 0:SROWS, :] + mix(lambda j: contact_ref[j, c, b])

        def finish(g, _):
            at = tile_rows(g)
            for b in range(halves):
                half = slice(b * BLK, (b + 1) * BLK)
                stiff, hard = stiff_ref[at, half], hard_ref[b, at, :]
                for c in range(comps):
                    u = u_ref[c, at, half] + mix(lambda j: x_ref[j, c, b, group_rows(g), :])
                    image = lu_ref[c, b, at, :] + mix(lambda j: l_ref[j, c, b, at, :])
                    bent = jnp.tanh(u / yield_scale)
                    material = stiff * (hard * u + (1.0 - hard) * yield_scale * bent)
                    residual = image + material - load_ref[c, at, half]
                    u_ref[c, at, half] = u
                    res_ref[c, at, half] = residual
                    lu_ref[c, b, at, :] = image
                    x_ref[0, c, b, group_rows(g), :] = -residual
                    d_ref[c, b, at, :] = stiff * (hard + (1.0 - hard) * (1.0 - bent * bent))
            return 0

        lax.fori_loop(0, groups, finish, 0)
        return 0

    lax.fori_loop(0, NEWTON, newton, 0)

    def drain(it, _):
        await_bytes(fsend.at[it, 0:n_zone - 1], fs.at[it])
        await_bytes(bsend.at[it, 0:(n_zone - 1) * CAP], bs.at[it])
        await_bytes(rsend.at[it], rs.at[it])
        await_bytes(csend.at[it], cs.at[it])
        await_bytes(srecv.at[it, 0:devices - 1], ss.at[it])
        return 0

    lax.fori_loop(0, STEPS, drain, 0)


def local(n_vol, n_zone, load, support_stiffness, plastic_flags, owner_map, pattern, active, mortar):
    comps, height, breadth = load.shape
    halves = breadth // BLK
    rows = active.shape[2]
    field = pltpu.VMEM((comps, halves, height, BLK), F32)
    slots = n_zone * CAP
    blocks = SROWS * halves
    devices = n_vol * n_zone
    dma = pltpu.SemaphoreType.DMA
    vmem = pl.BlockSpec(memory_space=pltpu.VMEM)
    hbm = pl.BlockSpec(memory_space=pltpu.HBM)
    flags = plastic_flags.T
    links = jnp.transpose(pattern, (0, 3, 1, 2))
    return pl.pallas_call(
        functools.partial(kernel, n_vol, n_zone),
        out_shape=[jax.ShapeDtypeStruct(load.shape, F32)] * 2,
        in_specs=[hbm] * 7,
        out_specs=[vmem, vmem],
        scratch_shapes=[
            pltpu.VMEM(load.shape, F32),
            pltpu.VMEM(support_stiffness.shape, F32),
            pltpu.VMEM(flags.shape, jnp.int32),
            pltpu.SMEM(owner_map.shape, jnp.int32),
            pltpu.SMEM(links.shape, jnp.int32),
            pltpu.SMEM(active.shape, jnp.int32),
            pltpu.VMEM(mortar.shape[2:], F32),
            pltpu.VMEM((KRY, comps, halves, height + 2 * PAD, BLK), F32),
            pltpu.VMEM((KRY, comps, halves, height, BLK), F32),
            field, field, field,
            pltpu.VMEM((halves, height, BLK), F32),
            pltpu.VMEM((KRY, comps, halves, SROWS, BLK), F32),
            pltpu.VMEM((KRY, rows * 8, BLK), F32),
            pltpu.VMEM((rows * 8, BLK), F32),
            pltpu.VMEM((rows, BLK, NNZ * BLK), BF16),
            pltpu.VMEM((rows, BLK, NNZ * BLK), BF16),
            pltpu.VMEM((slots * 4, rows * NNZ * 8), BF16),
            pltpu.VMEM((rows * NNZ * 8, BLK), F32),
            pltpu.VMEM((blocks * 8, BLK), F32),
            pltpu.VMEM((blocks + 1, 8, BLK), F32),
            pltpu.VMEM((blocks * 8, BLK), F32),
            pltpu.SMEM((slots,), jnp.int32),
            pltpu.SMEM((blocks,), jnp.int32),
            pltpu.VMEM((STEPS, n_zone, CAP, 4, BLK), F32),
            pltpu.VMEM((STEPS, slots, 4, BLK), F32),
            pltpu.VMEM((STEPS, slots, 4, BLK), F32),
            pltpu.VMEM((STEPS, slots, 4, BLK), F32),
            pltpu.VMEM((STEPS, 2, 8, BLK), F32),
            pltpu.VMEM((STEPS, 2, 8, BLK), F32),
            pltpu.VMEM((STEPS, 2, 8, BLK), F32),
            pltpu.VMEM((STEPS, 2, 8, BLK), F32),
            pltpu.VMEM((STEPS, 1, BLK), F32),
            pltpu.VMEM((STEPS, devices, 1, BLK), F32),
            dma((7,)),
        ] + [dma((STEPS,))] * 10,
        compiler_params=pltpu.CompilerParams(
            collective_id=0, has_side_effects=True, vmem_limit_bytes=32 * 1024 * 1024
        ),
    )(load, support_stiffness, flags, owner_map, links, active, mortar)


def solution(mesh):
    in_specs = (
        P(None, "vol", "zone"),
        P("vol", "zone"),
        P("vol", "zone"),
        P("vol", "zone", None),
        P("vol", "zone", None, None),
        P("vol", "zone", None),
        P("vol", "zone", None, None, None, None),
    )
    out_specs = (P(None, "vol", "zone"), P(None, "vol", "zone"))
    body = functools.partial(local, mesh.shape["vol"], mesh.shape["zone"])
    return jax.shard_map(body, mesh=mesh, in_specs=in_specs, out_specs=out_specs, check_vma=False)
```

time: 102 us -> 79.4 us (0.78)
  Pallas kernels: 93.4 us -> 70.6 us
    pallas_call x1, Pallas kernels: 93.4 us -> 70.6 us  [local(): pl.pallas_call(functools.partial(kernel, n_vol, n_zone), out_shape=[jax.S...]
    unnamed x14 -> x16, local copies, waits for them, and re-layouts: 8.13 us -> 7.94 us
where the time goes in v2:
time: 79.4 us; the launch traced here: 79.2 us
  Pallas kernels  70.6 us (89%)
  local copies, waits for them, and re-layouts  7.94 us (10%)
    pallas_call x1, Pallas kernels, local(): pl.pallas_call(functools.partial(kernel, n_vol, n_zone), out_shape=[jax.S...  70.6 us
    unnamed x16, local copies, waits for them, and re-layouts  7.94 us

profile of v2, /device:TPU:1, one launch (start us, length us, event | category | flops | bytes accessed | tf_op | source)
XLA Modules:
  0.0 79.2 jit_solution(4767316194986837756)
XLA Ops:
  0.6 0.0 copy-start
  0.6 1.9 %copy-done = f32[1,1,16,3,128,128]{5,4,3,2,1,0:T(8,128)S(1)} copy-done((f32[1,1,16,3,128,128]{5,4,3,2,1,0:T(8,128)S(1)}, f32[1,1,16,3,128,128]{5,4,3,2,1,0:T(8,128)}, u32[]{:S(2)}) %copy-start) | copy-done | bytes 3145752
  2.5 0.0 copy-start.1
  2.5 1.0 %copy-done.1 = f32[3,128,256]{2,1,0:T(8,128)S(1)} copy-done((f32[3,128,256]{2,1,0:T(8,128)S(1)}, f32[3,128,256]{2,1,0:T(8,128)}, u32[]{:S(2)}) %copy-start.1) | copy-done | bytes 393240
  3.5 0.0 copy-start.2
  3.5 0.9 %copy-done.2 = f32[128,256]{1,0:T(8,128)S(1)} copy-done((f32[128,256]{1,0:T(8,128)S(1)}, f32[128,256]{1,0:T(8,128)}, u32[]{:S(2)}) %copy-start.2) | copy-done | bytes 131096
  4.4 0.0 copy-start.3
  4.4 0.7 copy-done.3
  5.1 0.0 copy-start.4
  5.1 0.7 copy-done.4
  5.8 0.0 copy-start.5
  5.8 0.7 copy-done.5
  6.4 0.0 copy-start.6
  6.4 0.7 copy-done.6
  7.1 70.6 %shard_map.86 = (f32[3,128,256]{2,1,0:T(8,128)S(1)}, f32[3,128,256]{2,1,0:T(8,128)S(1)}) custom-call(f32[3,128,256]{2,1,0:T(8,128)S(1)} %copy-done.1, f32[128,256]{1,0:T(8,128)S(1)} %copy-done.2, s32[2,128]{1,0:T(2,128)S(1)} %bitcast.3, s32[1,1,16]{2,1,0:T(1,128)S(1)} %copy-done.5, s32[1,3,1,16]{3,2,1,0:T(1,128)S(1)} %bitcast.2, s32[1,1,16]{2,1,0:T(1,128)S(1)} %copy-done.6, ...), custom_call_target="tpu_custom_call" | custom-call | tf_op jit(solution)/shard_map/pallas_call | solution.py:469
  77.7 0.7 copy.11
  78.4 0.7 copy.12
Async XLA Ops:
  0.6 1.9 %copy-start = (f32[1,1,16,3,128,128]{5,4,3,2,1,0:T(8,128)S(1)}, f32[1,1,16,3,128,128]{5,4,3,2,1,0:T(8,128)}, u32[]{:S(2)}) copy-start(f32[1,1,16,3,128,128]{5,4,3,2,1,0:T(8,128)} %mortar_ref.1) | copy-start | bytes 9437188
  2.5 1.0 %copy-start.1 = (f32[3,128,256]{2,1,0:T(8,128)S(1)}, f32[3,128,256]{2,1,0:T(8,128)}, u32[]{:S(2)}) copy-start(f32[3,128,256]{2,1,0:T(8,128)} %load_hbm.1) | copy-start | bytes 1179652
  3.5 0.9 %copy-start.2 = (f32[128,256]{1,0:T(8,128)S(1)}, f32[128,256]{1,0:T(8,128)}, u32[]{:S(2)}) copy-start(f32[128,256]{1,0:T(8,128)} %stiff_hbm.1) | copy-start | bytes 393220
  4.4 0.7 copy-start.3
  5.1 0.7 copy-start.4
  5.8 0.7 copy-start.5
  6.4 0.7 copy-start.6

commit v3 on v2

--- a/solution.py
+++ b/solution.py
@@ -508,7 +508,7 @@
             dma((7,)),
         ] + [dma((STEPS,))] * 10,
         compiler_params=pltpu.CompilerParams(
-            collective_id=0, has_side_effects=True, vmem_limit_bytes=32 * 1024 * 1024
+            collective_id=0, has_side_effects=True, vmem_limit_bytes=60 * 1024 * 1024
         ),
     )(load, support_stiffness, flags, owner_map, links, active, mortar)
 

time: 79.4 us -> 75.4 us (0.950)
  local copies, waits for them, and re-layouts: 7.94 us -> 3.53 us
    unnamed x16 -> x2, local copies, waits for them, and re-layouts: 7.94 us -> 3.53 us
where the time goes in v3:
time: 75.4 us; the launch traced here: 75.2 us
  Pallas kernels  71 us (94%)
  local copies, waits for them, and re-layouts  3.53 us (5%)
    pallas_call x1, Pallas kernels, local(): pl.pallas_call(functools.partial(kernel, n_vol, n_zone), out_shape=[jax.S...  71 us
    unnamed x2, local copies, waits for them, and re-layouts  3.53 us

profile of v3, /device:TPU:1, one launch (start us, length us, event | category | flops | bytes accessed | tf_op | source)
XLA Modules:
  0.0 75.2 jit_solution(14147533233107592136)
XLA Ops:
  0.6 71.0 %shard_map.86 = (f32[3,128,256]{2,1,0:T(8,128)}, f32[3,128,256]{2,1,0:T(8,128)}) custom-call(f32[3,128,256]{2,1,0:T(8,128)} %load_hbm.1, f32[128,256]{1,0:T(8,128)} %stiff_hbm.1, s32[2,128]{1,0:T(2,128)} %bitcast.3, s32[1,1,16]{2,1,0:T(1,128)} %owner_hbm.1, s32[1,3,1,16]{3,2,1,0:T(1,128)} %bitcast.2, s32[1,1,16]{2,1,0:T(1,128)} %active_hbm.1, ...), custom_call_target="tpu_custom_call" | custom-call | tf_op jit(solution)/shard_map/pallas_call | solution.py:469
  71.6 1.8 %copy.11 = f32[3,128,256]{2,1,0:T(8,128)} copy(f32[3,128,256]{2,1,0:T(8,128)} %get-tuple-element.4) | data formatting | bytes 786432
  73.4 1.8 %copy.12 = f32[3,128,256]{2,1,0:T(8,128)} copy(f32[3,128,256]{2,1,0:T(8,128)} %get-tuple-element.5) | data formatting | bytes 786432

commit v4 on v2

--- a/solution.py
+++ b/solution.py
@@ -33,9 +33,10 @@
     mhi_ref, mlo_ref, spread_ref, push_ref,
     surf_ref, block_ref, back_ref,
     pack_tab, unpack_tab,
-    fsend, frecv, bsend, brecv, rsend, rrecv, csend, crecv, ssend, srecv,
+    fsend, frecv0, frecv1, frecv2, bsend, brecv0, brecv1, brecv2, rsend, rrecv, csend, crecv, ssend, srecv,
     in_sem, fs, fr, bs, br, rs, rr, cs, cr, ss, sr,
 ):
+    frecv, brecv = (frecv0, frecv1, frecv2), (brecv0, brecv1, brecv2)
     comps, height = load_ref.shape[0], load_ref.shape[1]
     halves = load_ref.shape[2] // BLK
     groups = height // 8
@@ -169,10 +170,11 @@
 
         return lax.fori_loop(0, groups, group, init, unroll=2)
 
-    def send_field(j, it):
+    def send_surface(j, n, tile):
+        it = n * KRY + j
         for c in range(comps):
             for b in range(halves):
-                surf_ref[pl.ds(b * 8 + c, SROWS, stride=8 * halves), :] = x_ref[j, c, b, PAD:PAD + SROWS, :]
+                surf_ref[pl.ds(b * 8 + c, SROWS, stride=8 * halves), :] = tile(c, b)
         for m in range(blocks):
             block_ref[m] = surf_ref[m * 8:m * 8 + 8, :]
         for step in (4, 3, 5, 2, 6, 1, 7, 0):
@@ -182,11 +184,22 @@
                 if step:
                     fsend[it, step, k] = block
                 else:
-                    frecv[it, zone * CAP + k] = block
+                    frecv[j][n, zone * CAP + k] = block
             if step:
                 remote(
-                    fsend.at[it, step], frecv.at[it, slots_of(zone)], fs.at[it], fr.at[it], {"zone": z}
+                    fsend.at[it, step], frecv[j].at[n, slots_of(zone)], fs.at[it], fr.at[it], {"zone": z}
                 ).start()
+
+    def field_surface(n):
+        send_surface(0, n, lambda c, b: x_ref[0, c, b, PAD:PAD + SROWS, :])
+
+    def grid_surface(j, n):
+        send_surface(
+            j + 1, n,
+            lambda c, b: l_ref[j, c, b, 0:SROWS, :] + d_ref[c, b, 0:SROWS, :] * x_ref[j, c, b, PAD:PAD + SROWS, :],
+        )
+
+    def send_halo(j, it):
         for c in range(comps):
             for b in range(halves):
                 i = c * halves + b
@@ -247,26 +260,36 @@
     upper = lax.broadcasted_iota(jnp.int32, (8, NNZ * BLK), 0) < 4
     contract_last = (((1,), (1,)), ((), ()))
 
-    def split_rows(both, mask):
-        high = both.astype(BF16).astype(F32)
-        return jnp.where(mask, high, both - high).astype(BF16)
-
-    def find_gaps(j, it):
-        await_bytes(frecv.at[it, 0:(n_zone - 1) * CAP], fr.at[it])
+    def split_rows(piece):
+        high = piece.astype(BF16).astype(F32)
+        rest = piece - high
+        middle = rest.astype(BF16).astype(F32)
+        return jnp.concatenate([high, middle, rest - middle, jnp.zeros_like(piece)], axis=0).astype(BF16)
+
+    def join_rows(product):
+        product = product[0:8] + product[8:16]
+        return product + pltpu.roll(product, 4, axis=0)
+
+    def find_gaps(j, n):
+        it = n * KRY + j
+        await_bytes(frecv[j].at[n, 0:(n_zone - 1) * CAP], fr.at[it])
         for r in range(rows):
-            picked = jnp.concatenate([frecv[it, link(r, k)] for k in range(NNZ)], axis=1)
-            picked = split_rows(jnp.concatenate([picked, picked], axis=0), upper)
+            picked = jnp.concatenate([frecv[j][n, link(r, k)] for k in range(NNZ)], axis=1)
+            if j:
+                picked = picked + jnp.concatenate([bsend[it - 1, link(r, k)] for k in range(NNZ)], axis=1)
+            picked = split_rows(picked)
             gap = lax.dot_general(picked, mhi_ref[r], contract_last, preferred_element_type=F32)
             gap = gap + lax.dot_general(picked, mlo_ref[r], contract_last, preferred_element_type=F32)
-            gap_ref[j, r * 8:r * 8 + 8, :] = gap + pltpu.roll(gap, 4, axis=0)
-
-    def push_forces(j, it):
+            gap_ref[j, r * 8:r * 8 + 8, :] = join_rows(gap)
+
+    def push_forces(j, n):
+        it = n * KRY + j
         for r in range(rows):
             at = slice(r * 8, r * 8 + 8)
-            multiplier = split_rows(scale_ref[at, :] * gap_ref[j, at, :], sub < 4)
+            multiplier = split_rows((scale_ref[at, :] * gap_ref[j, at, :])[0:4])
             force = jnp.dot(multiplier, mhi_ref[r], preferred_element_type=F32)
             force = force + jnp.dot(multiplier, mlo_ref[r], preferred_element_type=F32)
-            force = force + pltpu.roll(force, 4, axis=0)
+            force = join_rows(force)
             high = force.astype(BF16).astype(F32)
             force = jnp.where(upper, high, force - high)
             for k in range(NNZ):
@@ -277,14 +300,14 @@
         for step in (4, 3, 5, 2, 6, 1, 7):
             z = at_zone(step)
             remote(
-                bsend.at[it, slots_of(z)], brecv.at[it, slots_of(zone)], bs.at[it], br.at[it], {"zone": z}
+                bsend.at[it, slots_of(z)], brecv[j].at[n, slots_of(zone)], bs.at[it], br.at[it], {"zone": z}
             ).start()
-        brecv[it, slots_of(zone)] = bsend[it, slots_of(zone)]
-
-    def receive_forces(j, it):
-        await_bytes(brecv.at[it, 0:(n_zone - 1) * CAP], br.at[it])
+        brecv[j][n, slots_of(zone)] = bsend[it, slots_of(zone)]
+
+    def receive_forces(j, n):
+        await_bytes(brecv[j].at[n, 0:(n_zone - 1) * CAP], br.at[n * KRY + j])
         for m in range(blocks):
-            back_ref[m * 8:m * 8 + 4, :] = brecv[it, unpack_tab[m]]
+            back_ref[m * 8:m * 8 + 4, :] = brecv[j][n, unpack_tab[m]]
         for c in range(comps):
             for b in range(halves):
                 contact_ref[j, c, b] = back_ref[pl.ds(b * 8 + c, SROWS, stride=8 * halves), :]
@@ -322,13 +345,6 @@
     def full(scalar):
         return jnp.broadcast_to(scalar, (8, BLK))
 
-    def next_field(j):
-        def tile(c, b, padded, at, _):
-            x_ref[j + 1, c, b, padded, :] = l_ref[j, c, b, at, :] + d_ref[c, b, at, :] * x_ref[j, c, b, padded, :]
-            return 0
-
-        over_tiles(tile, 0)
-
     def add_contact(j):
         for c in range(comps):
             for b in range(halves):
@@ -338,11 +354,12 @@
     def newton(n, _):
         it = n * KRY
 
-        send_field(0, it)
+        send_halo(0, it)
         inner(0)
-        find_gaps(0, it)
-        push_forces(0, it)
+        find_gaps(0, n)
+        push_forces(0, n)
         outer(0, it)
+        grid_surface(0, n)
 
         def dots0(c, b, padded, at, sums):
             x = x_ref[0, c, b, padded, :]
@@ -352,16 +369,16 @@
 
         gamma, delta = over_tiles(dots0, (zero, zero))
         start_sums(it, gamma, delta + energy(lambda at: gap_ref[0, at, :]), zero)
-        receive_forces(0, it)
+        receive_forces(0, n)
         add_contact(0)
-
-        send_field(1, it + 1)
+        send_halo(1, it + 1)
         inner(1)
+        find_gaps(1, n)
+        push_forces(1, n)
         gamma0, pq0, _ = finish_sums(it)
         a0 = gamma0 / pq0
-        find_gaps(1, it + 1)
-        push_forces(1, it + 1)
         outer(1, it + 1)
+        grid_surface(1, n)
         w0 = full(a0)
 
         def dots1(c, b, padded, at, sums):
@@ -374,17 +391,16 @@
 
         gamma, delta, cross = over_tiles(dots1, (zero, zero, zero))
         start_sums(it + 1, gamma, delta + energy(lambda at: gap_ref[0, at, :] - w0 * gap_ref[1, at, :]), cross)
-        receive_forces(1, it + 1)
+        receive_forces(1, n)
         add_contact(1)
-
-        send_field(2, it + 2)
+        send_halo(2, it + 2)
         inner(2)
+        find_gaps(2, n)
+        outer(2, it + 2)
         gamma1, delta, cross = finish_sums(it + 1)
         beta1 = gamma1 / gamma0
         pq1 = delta + beta1 * (2.0 * cross + beta1 * pq0)
         a1 = gamma1 / pq1
-        find_gaps(2, it + 2)
-        outer(2, it + 2)
         more, w1 = full(1.0 + beta1), full(a1)
 
         def second(x0, x1, x2):
@@ -401,8 +417,8 @@
         gamma, delta, cross = over_tiles(dots2, (zero, zero, zero))
         stored = energy(lambda at: second(gap_ref[0, at, :], gap_ref[1, at, :], gap_ref[2, at, :])[1])
         start_sums(it + 2, gamma, delta + stored, cross)
-        push_forces(2, it + 2)
-        receive_forces(2, it + 2)
+        push_forces(2, n)
+        receive_forces(2, n)
         gamma2, delta, cross = finish_sums(it + 2)
         beta2 = gamma2 / gamma1
         pq2 = delta + beta2 * (2.0 * cross + beta2 * pq1)
@@ -437,9 +453,16 @@
                     d_ref[c, b, at, :] = stiff * (hard + (1.0 - hard) * (1.0 - bent * bent))
             return 0
 
-        lax.fori_loop(0, groups, finish, 0)
+        finish(0, 0)
+
+        @pl.when(n < NEWTON - 1)
+        def _():
+            field_surface(n + 1)
+
+        lax.fori_loop(1, groups, finish, 0)
         return 0
 
+    field_surface(0)
     lax.fori_loop(0, NEWTON, newton, 0)
 
     def drain(it, _):
@@ -459,6 +482,7 @@
     rows = active.shape[2]
     field = pltpu.VMEM((comps, halves, height, BLK), F32)
     slots = n_zone * CAP
+    landing = pltpu.VMEM((NEWTON, slots, 4, BLK), F32)
     blocks = SROWS * halves
     devices = n_vol * n_zone
     dma = pltpu.SemaphoreType.DMA
@@ -466,6 +490,7 @@
     hbm = pl.BlockSpec(memory_space=pltpu.HBM)
     flags = plastic_flags.T
     links = jnp.transpose(pattern, (0, 3, 1, 2))
+    operands = (load, support_stiffness, flags, owner_map, links, active, mortar)
     return pl.pallas_call(
         functools.partial(kernel, n_vol, n_zone),
         out_shape=[jax.ShapeDtypeStruct(load.shape, F32)] * 2,
@@ -496,9 +521,9 @@
             pltpu.SMEM((slots,), jnp.int32),
             pltpu.SMEM((blocks,), jnp.int32),
             pltpu.VMEM((STEPS, n_zone, CAP, 4, BLK), F32),
+            landing, landing, landing,
             pltpu.VMEM((STEPS, slots, 4, BLK), F32),
-            pltpu.VMEM((STEPS, slots, 4, BLK), F32),
-            pltpu.VMEM((STEPS, slots, 4, BLK), F32),
+            landing, landing, landing,
             pltpu.VMEM((STEPS, 2, 8, BLK), F32),
             pltpu.VMEM((STEPS, 2, 8, BLK), F32),
             pltpu.VMEM((STEPS, 2, 8, BLK), F32),
@@ -510,7 +535,7 @@
         compiler_params=pltpu.CompilerParams(
             collective_id=0, has_side_effects=True, vmem_limit_bytes=32 * 1024 * 1024
         ),
-    )(load, support_stiffness, flags, owner_map, links, active, mortar)
+    )(*[pltpu.with_memory_space_constraint(a, pltpu.HBM) for a in operands])
 
 
 def solution(mesh):

time: 79.4 us -> 67.3 us (0.85)
  local copies, waits for them, and re-layouts: 7.94 us -> 1.49 us
  Pallas kernels: 70.6 us -> 65.1 us
    unnamed x16 -> x2, local copies, waits for them, and re-layouts: 7.94 us -> 1.49 us
    pallas_call x1, Pallas kernels: 70.6 us -> 65.1 us  [local(): pl.pallas_call(functools.partial(kernel, n_vol, n_zone), out_shape=[jax.S...]
where the time goes in v4:
time: 67.3 us; the launch traced here: 67.2 us
  Pallas kernels  65.1 us (97%)
  local copies, waits for them, and re-layouts  1.49 us (2%)
    pallas_call x1, Pallas kernels, local(): pl.pallas_call(functools.partial(kernel, n_vol, n_zone), out_shape=[jax.S...  65.1 us
    unnamed x2, local copies, waits for them, and re-layouts  1.49 us

profile of v4, /device:TPU:1, one launch (start us, length us, event | category | flops | bytes accessed | tf_op | source)
XLA Modules:
  0.0 67.2 jit_solution(135499487753263243)
XLA Ops:
  0.6 65.1 %shard_map.86 = (f32[3,128,256]{2,1,0:T(8,128)S(1)}, f32[3,128,256]{2,1,0:T(8,128)S(1)}) custom-call(f32[3,128,256]{2,1,0:T(8,128)} %load_hbm.1, f32[128,256]{1,0:T(8,128)} %stiff_hbm.1, s32[2,128]{1,0:T(2,128)} %bitcast.3, s32[1,1,16]{2,1,0:T(1,128)} %owner_hbm.1, s32[1,3,1,16]{3,2,1,0:T(1,128)} %bitcast.2, s32[1,1,16]{2,1,0:T(1,128)} %active_hbm.1, ...), custom_call_target="tpu_custom_call" | custom-call | tf_op jit(solution)/shard_map/pallas_call | solution.py:494
  65.7 0.7 %copy.11 = f32[3,128,256]{2,1,0:T(8,128)} copy(f32[3,128,256]{2,1,0:T(8,128)S(1)} %get-tuple-element.4) | data formatting | bytes 786432
  66.4 0.7 %copy.12 = f32[3,128,256]{2,1,0:T(8,128)} copy(f32[3,128,256]{2,1,0:T(8,128)S(1)} %get-tuple-element.5) | data formatting | bytes 786432

commit v5 on v4

--- a/solution.py
+++ b/solution.py
@@ -29,7 +29,7 @@
     load_hbm, stiff_hbm, flags_hbm, owner_hbm, pattern_hbm, active_hbm, mortar_ref,
     u_ref, res_ref,
     load_ref, stiff_ref, flags_ref, owner_ref, pattern_ref, active_ref, mort_ref,
-    x_ref, l_ref, r_ref, d_ref, lu_ref, hard_ref, contact_ref, gap_ref, scale_ref,
+    x_ref, l_ref, r_ref, d_ref, lu_ref, hard_ref, contact_ref, halo_ref, gap_ref, scale_ref,
     mhi_ref, mlo_ref, spread_ref, push_ref,
     surf_ref, block_ref, back_ref,
     pack_tab, unpack_tab,
@@ -100,27 +100,9 @@
     def link(r, k):
         return pattern_ref[0, k, 0, r]
 
-    wide = rows * NNZ * 8
-    link_lane = lax.broadcasted_iota(jnp.int32, (1, wide), 1)
-    links = jnp.zeros((1, wide), jnp.int32)
-    for r in range(rows):
-        scale_ref[r * 8:r * 8 + 8, :] = jnp.full((8, BLK), penalty * active_ref[0, 0, r].astype(F32))
-        for k in range(NNZ):
-            links = jnp.where(link_lane // 8 == r * NNZ + k, link(r, k), links)
-    out_row = lax.broadcasted_iota(jnp.int32, (n_zone * CAP * 4, wide), 0)
-    out_lane = lax.broadcasted_iota(jnp.int32, (n_zone * CAP * 4, wide), 1)
-    hit = (out_row // 4 == links) & (lax.rem(out_row, 4) == lax.rem(out_lane, 4))
-    spread_ref[...] = jnp.where(hit, 1.0, 0.0).astype(BF16)
-
     surf_ref[...] = jnp.zeros_like(surf_ref)
     block_ref[blocks] = zero
-    back_ref[...] = jnp.zeros_like(back_ref)
     rsend[...] = jnp.zeros_like(rsend)
-    u_ref[...] = jnp.zeros_like(u_ref)
-    lu_ref[...] = jnp.zeros_like(lu_ref)
-    for b in range(halves):
-        flag = jnp.transpose(jnp.broadcast_to(flags_ref[b:b + 1, :], (height, BLK)))
-        hard_ref[b] = jnp.where(flag == 1, plastic_hardening, 1.0).astype(F32)
     for fetch in fetches[4:6]:
         fetch.wait()
     for c in range(comps):
@@ -130,7 +112,6 @@
                 x_ref[j, c, b, PAD + height:, :] = jnp.zeros((PAD, BLK), F32)
             x_ref[0, c, b, PAD:PAD + height, :] = load_ref[c, :, b * BLK:(b + 1) * BLK]
             d_ref[c, b] = stiff_ref[:, b * BLK:(b + 1) * BLK]
-    fetches[6].wait()
 
     def split(r, _):
         for k in range(NNZ):
@@ -140,7 +121,30 @@
             mlo_ref[r, :, k * BLK:(k + 1) * BLK] = (piece - high.astype(F32)).astype(BF16)
         return 0
 
-    lax.fori_loop(0, rows, split, 0)
+    def set_up():
+        pairs = rows * NNZ * 8
+        wide = push_ref.shape[0]
+        link_lane = lax.broadcasted_iota(jnp.int32, (1, wide), 1)
+        tail = (link_lane - pairs) // 4
+        entry = jnp.where(link_lane < pairs, link_lane // 8, jnp.where(tail < rows * NNZ, tail, -1))
+        links = jnp.full((1, wide), -1, jnp.int32)
+        for r in range(rows):
+            scale_ref[r * 8:r * 8 + 8, :] = jnp.full((8, BLK), penalty * active_ref[0, 0, r].astype(F32))
+            for k in range(NNZ):
+                links = jnp.where(entry == r * NNZ + k, link(r, k), links)
+        out_row = lax.broadcasted_iota(jnp.int32, (n_zone * CAP * 4, wide), 0)
+        out_lane = lax.broadcasted_iota(jnp.int32, (n_zone * CAP * 4, wide), 1)
+        hit = (out_row // 4 == links) & (lax.rem(out_row, 4) == lax.rem(out_lane, 4))
+        spread_ref[...] = jnp.where(hit, 1.0, 0.0).astype(BF16)
+        back_ref[...] = jnp.zeros_like(back_ref)
+        push_ref[...] = jnp.zeros_like(push_ref)
+        u_ref[...] = jnp.zeros_like(u_ref)
+        lu_ref[...] = jnp.zeros_like(lu_ref)
+        for b in range(halves):
+            flag = jnp.transpose(jnp.broadcast_to(flags_ref[b:b + 1, :], (height, BLK)))
+            hard_ref[b] = jnp.where(flag == 1, plastic_hardening, 1.0).astype(F32)
+        fetches[6].wait()
+        lax.fori_loop(0, rows, split, 0)
 
     pl.semaphore_wait(barrier, devices - 1)
 
@@ -170,11 +174,11 @@
 
         return lax.fori_loop(0, groups, group, init, unroll=2)
 
-    def send_surface(j, n, tile):
+    def send_surface(j, n):
         it = n * KRY + j
         for c in range(comps):
             for b in range(halves):
-                surf_ref[pl.ds(b * 8 + c, SROWS, stride=8 * halves), :] = tile(c, b)
+                surf_ref[pl.ds(b * 8 + c, SROWS, stride=8 * halves), :] = x_ref[j, c, b, PAD:PAD + SROWS, :]
         for m in range(blocks):
             block_ref[m] = surf_ref[m * 8:m * 8 + 8, :]
         for step in (4, 3, 5, 2, 6, 1, 7, 0):
@@ -190,23 +194,18 @@
                     fsend.at[it, step], frecv[j].at[n, slots_of(zone)], fs.at[it], fr.at[it], {"zone": z}
                 ).start()
 
-    def field_surface(n):
-        send_surface(0, n, lambda c, b: x_ref[0, c, b, PAD:PAD + SROWS, :])
-
-    def grid_surface(j, n):
-        send_surface(
-            j + 1, n,
-            lambda c, b: l_ref[j, c, b, 0:SROWS, :] + d_ref[c, b, 0:SROWS, :] * x_ref[j, c, b, PAD:PAD + SROWS, :],
-        )
-
-    def send_halo(j, it):
+    def send_row(j, it, end):
+        at = PAD + (height - 1 if end else 0)
         for c in range(comps):
             for b in range(halves):
                 i = c * halves + b
-                rsend[it, 0, i:i + 1, :] = x_ref[j, c, b, PAD:PAD + 1, :]
-                rsend[it, 1, i:i + 1, :] = x_ref[j, c, b, PAD + height - 1:PAD + height, :]
-        remote(rsend.at[it, 0], rrecv.at[it, 1], rs.at[it], rr.at[it], {"vol": at_vol(n_vol - 1)}).start()
-        remote(rsend.at[it, 1], rrecv.at[it, 0], rs.at[it], rr.at[it], {"vol": at_vol(1)}).start()
+                rsend[it, end, i:i + 1, :] = x_ref[j, c, b, at:at + 1, :]
+        target = at_vol(1 if end else n_vol - 1)
+        remote(
+            rsend.at[it, end], rrecv.at[it, 1 - end], rs.at[it, end], rr.at[it, 1 - end], {"vol": target}
+        ).start()
+
+    def send_strips(j, it):
         for end, b, column in ((0, 0, 0), (1, halves - 1, BLK - 1)):
             strip = zero
             for c in range(comps):
@@ -218,6 +217,32 @@
             csend[it, end] = strip
         remote(csend.at[it, 0], crecv.at[it, 1], cs.at[it], cr.at[it], {"zone": at_zone(n_zone - 1)}).start()
         remote(csend.at[it, 1], crecv.at[it, 0], cs.at[it], cr.at[it], {"zone": at_zone(1)}).start()
+
+    def take_row(j, it, end):
+        await_bytes(rrecv.at[it, end], rr.at[it, end])
+        halo_ref[j, end] = jnp.where(vol == (n_vol - 1 if end else 0), 0.0, rrecv[it, end])
+
+    def take_strips(j, it):
+        await_bytes(crecv.at[it], cr.at[it])
+        halo_ref[j, 2] = jnp.where(zone == 0, 0.0, crecv[it, 0])
+        halo_ref[j, 3] = jnp.where(zone == n_zone - 1, 0.0, crecv[it, 1])
+
+    def apply_row(field, offset, end, halo):
+        at = offset + (height - 1 if end else 0)
+        for c in range(comps):
+            for b in range(halves):
+                i = c * halves + b
+                field[c, b, at:at + 1, :] = field[c, b, at:at + 1, :] - halo[i:i + 1]
+
+    def apply_strips(field, offset, left, right, chosen):
+        for halo, b, column in ((left, 0, 0), (right, halves - 1, BLK - 1)):
+            for c in range(comps):
+                for g in chosen:
+                    i = c * groups + g
+                    at = slice(offset + g * 8, offset + g * 8 + 8)
+                    spread = jnp.broadcast_to(halo[:, i:i + 1], (8, BLK))
+                    image = field[c, b, at, :]
+                    field[c, b, at, :] = jnp.where(lane == column, image - spread, image)
 
     def inner(j):
         def group(g, _):
@@ -237,25 +262,29 @@
 
         lax.fori_loop(0, groups, group, 0, unroll=2)
 
-    def outer(j, it):
-        await_bytes(rrecv.at[it], rr.at[it])
-        await_bytes(crecv.at[it], cr.at[it])
-        over = jnp.where(vol == 0, 0.0, rrecv[it, 0])
-        under = jnp.where(vol == n_vol - 1, 0.0, rrecv[it, 1])
-        left = jnp.where(zone == 0, 0.0, crecv[it, 0])
-        right = jnp.where(zone == n_zone - 1, 0.0, crecv[it, 1])
+    def first_rows(j):
         for c in range(comps):
             for b in range(halves):
-                i = c * halves + b
-                l_ref[j, c, b, 0:1, :] = l_ref[j, c, b, 0:1, :] - over[i:i + 1]
-                l_ref[j, c, b, height - 1:height, :] = l_ref[j, c, b, height - 1:height, :] - under[i:i + 1]
-        for halo, b, column in ((left, 0, 0), (right, halves - 1, BLK - 1)):
+                at = slice(PAD, PAD + SROWS)
+                x_ref[j + 1, c, b, at, :] = l_ref[j, c, b, 0:SROWS, :] + d_ref[c, b, 0:SROWS, :] * x_ref[j, c, b, at, :]
+        field = x_ref.at[j + 1]
+        apply_row(field, PAD, 0, halo_ref[j, 0])
+        apply_strips(field, PAD, halo_ref[j, 2], halo_ref[j, 3], range(1))
+
+    def other_rows(j):
+        def group(g, _):
             for c in range(comps):
-                for g in range(groups):
-                    i = c * groups + g
-                    spread = jnp.broadcast_to(halo[:, i:i + 1], (8, BLK))
-                    image = l_ref[j, c, b, g * 8:g * 8 + 8, :]
-                    l_ref[j, c, b, g * 8:g * 8 + 8, :] = jnp.where(lane == column, image - spread, image)
+                for b in range(halves):
+                    x = x_ref[j, c, b, group_rows(g), :]
+                    x_ref[j + 1, c, b, group_rows(g), :] = (
+                        l_ref[j, c, b, tile_rows(g), :] + d_ref[c, b, tile_rows(g), :] * x
+                    )
+            return 0
+
+        lax.fori_loop(1, groups, group, 0, unroll=3)
+        field = x_ref.at[j + 1]
+        apply_row(field, PAD, 1, halo_ref[j, 1])
+        apply_strips(field, PAD, halo_ref[j, 2], halo_ref[j, 3], range(1, groups))
 
     upper = lax.broadcasted_iota(jnp.int32, (8, NNZ * BLK), 0) < 4
     contract_last = (((1,), (1,)), ((), ()))
@@ -291,10 +320,16 @@
             force = force + jnp.dot(multiplier, mlo_ref[r], preferred_element_type=F32)
             force = join_rows(force)
             high = force.astype(BF16).astype(F32)
-            force = jnp.where(upper, high, force - high)
+            rest = force - high
+            middle = rest.astype(BF16).astype(F32)
+            two = jnp.where(upper, high, middle)
+            low = (rest - middle)[0:4]
             for k in range(NNZ):
-                to = (r * NNZ + k) * 8
-                push_ref[to:to + 8, :] = force[:, k * BLK:(k + 1) * BLK]
+                entry = r * NNZ + k
+                part = slice(k * BLK, (k + 1) * BLK)
+                push_ref[entry * 8:entry * 8 + 8, :] = two[:, part]
+                to = rows * NNZ * 8 + entry * 4
+                push_ref[to:to + 4, :] = low[:, part]
         summed = jnp.dot(spread_ref[...], push_ref[...].astype(BF16), preferred_element_type=F32)
         bsend[it] = summed.reshape(n_zone * CAP, 4, BLK)
         for step in (4, 3, 5, 2, 6, 1, 7):
@@ -351,34 +386,47 @@
                 at = slice(PAD, PAD + SROWS)
                 x_ref[j + 1, c, b, at, :] = x_ref[j + 1, c, b, at, :] + contact_ref[j, c, b]
 
+    def edges(mix):
+        return 2.0 * (
+            mix(lambda j, it: rsend[it + j, 0]) * mix(lambda j, it: halo_ref[j, 0])
+            + mix(lambda j, it: csend[it + j, 0]) * mix(lambda j, it: halo_ref[j, 2])
+        )
+
     def newton(n, _):
         it = n * KRY
 
-        send_halo(0, it)
         inner(0)
         find_gaps(0, n)
         push_forces(0, n)
-        outer(0, it)
-        grid_surface(0, n)
+        take_row(0, it, 0)
+        take_strips(0, it)
+        first_rows(0)
+        send_surface(1, n)
 
         def dots0(c, b, padded, at, sums):
             x = x_ref[0, c, b, padded, :]
             q = l_ref[0, c, b, at, :] + d_ref[c, b, at, :] * x
-            x_ref[1, c, b, padded, :] = q
             return sums[0] + x * x, sums[1] + x * q
 
         gamma, delta = over_tiles(dots0, (zero, zero))
-        start_sums(it, gamma, delta + energy(lambda at: gap_ref[0, at, :]), zero)
+        delta = delta + energy(lambda at: gap_ref[0, at, :]) - edges(lambda part: part(0, it))
+        start_sums(it, gamma, delta, zero)
+        take_row(0, it, 1)
+        other_rows(0)
+        send_row(1, it + 1, 1)
         receive_forces(0, n)
         add_contact(0)
-        send_halo(1, it + 1)
+        send_strips(1, it + 1)
+        send_row(1, it + 1, 0)
         inner(1)
         find_gaps(1, n)
         push_forces(1, n)
         gamma0, pq0, _ = finish_sums(it)
         a0 = gamma0 / pq0
-        outer(1, it + 1)
-        grid_surface(1, n)
+        take_row(1, it + 1, 0)
+        take_strips(1, it + 1)
+        first_rows(1)
+        send_surface(2, n)
         w0 = full(a0)
 
         def dots1(c, b, padded, at, sums):
@@ -386,38 +434,45 @@
             r = x_ref[0, c, b, padded, :] - w0 * x1
             r_ref[c, b, at, :] = r
             q = (l_ref[0, c, b, at, :] - w0 * l_ref[1, c, b, at, :]) + d_ref[c, b, at, :] * r
-            x_ref[2, c, b, padded, :] = l_ref[1, c, b, at, :] + d_ref[c, b, at, :] * x1
             return sums[0] + r * r, sums[1] + r * q, sums[2] + r * x1
 
         gamma, delta, cross = over_tiles(dots1, (zero, zero, zero))
-        start_sums(it + 1, gamma, delta + energy(lambda at: gap_ref[0, at, :] - w0 * gap_ref[1, at, :]), cross)
+        delta = delta + energy(lambda at: gap_ref[0, at, :] - w0 * gap_ref[1, at, :])
+        delta = delta - edges(lambda part: part(0, it) - w0 * part(1, it))
+        start_sums(it + 1, gamma, delta, cross)
+        take_row(1, it + 1, 1)
+        other_rows(1)
+        send_row(2, it + 2, 1)
         receive_forces(1, n)
         add_contact(1)
-        send_halo(2, it + 2)
+        send_strips(2, it + 2)
+        send_row(2, it + 2, 0)
         inner(2)
         find_gaps(2, n)
-        outer(2, it + 2)
         gamma1, delta, cross = finish_sums(it + 1)
         beta1 = gamma1 / gamma0
         pq1 = delta + beta1 * (2.0 * cross + beta1 * pq0)
         a1 = gamma1 / pq1
+        take_row(2, it + 2, 0)
+        take_strips(2, it + 2)
         more, w1 = full(1.0 + beta1), full(a1)
 
         def second(x0, x1, x2):
-            image = more * x1 - w0 * x2
-            return image, (x0 - w0 * x1) - w1 * image
+            return (x0 - w0 * x1) - w1 * (more * x1 - w0 * x2)
 
         def dots2(c, b, padded, at, sums):
             image = more * x_ref[1, c, b, padded, :] - w0 * x_ref[2, c, b, padded, :]
             r = r_ref[c, b, at, :] - w1 * image
-            _, q = second(l_ref[0, c, b, at, :], l_ref[1, c, b, at, :], l_ref[2, c, b, at, :])
+            q = second(l_ref[0, c, b, at, :], l_ref[1, c, b, at, :], l_ref[2, c, b, at, :])
             q = q + d_ref[c, b, at, :] * r
             return sums[0] + r * r, sums[1] + r * q, sums[2] + r * image
 
         gamma, delta, cross = over_tiles(dots2, (zero, zero, zero))
-        stored = energy(lambda at: second(gap_ref[0, at, :], gap_ref[1, at, :], gap_ref[2, at, :])[1])
-        start_sums(it + 2, gamma, delta + stored, cross)
+        delta = delta + energy(lambda at: second(gap_ref[0, at, :], gap_ref[1, at, :], gap_ref[2, at, :]))
+        delta = delta - edges(lambda part: second(part(0, it), part(1, it), part(2, it)))
+        start_sums(it + 2, gamma, delta, cross)
         push_forces(2, n)
+        take_row(2, it + 2, 1)
         receive_forces(2, n)
         gamma2, delta, cross = finish_sums(it + 2)
         beta2 = gamma2 / gamma1
@@ -434,6 +489,9 @@
         for c in range(comps):
             for b in range(halves):
                 lu_ref[c, b, 0:SROWS, :] = lu_ref[c, b, 0:SROWS, :] + mix(lambda j: contact_ref[j, c, b])
+        over, under, left, right = [mix(lambda j: halo_ref[j, i]) for i in range(4)]
+        apply_row(lu_ref, 0, 0, over)
+        apply_strips(lu_ref, 0, left, right, range(1))
 
         def finish(g, _):
             at = tile_rows(g)
@@ -457,18 +515,33 @@
 
         @pl.when(n < NEWTON - 1)
         def _():
-            field_surface(n + 1)
-
+            send_surface(0, n + 1)
+
+        apply_row(lu_ref, 0, 1, under)
+        apply_strips(lu_ref, 0, left, right, range(1, groups))
         lax.fori_loop(1, groups, finish, 0)
+
+        @pl.when(n < NEWTON - 1)
+        def _():
+            send_outline(it + KRY)
+
         return 0
 
-    field_surface(0)
+    def send_outline(it):
+        send_row(0, it, 1)
+        send_row(0, it, 0)
+        send_strips(0, it)
+
+    send_surface(0, 0)
+    send_outline(0)
+    set_up()
     lax.fori_loop(0, NEWTON, newton, 0)
 
     def drain(it, _):
         await_bytes(fsend.at[it, 0:n_zone - 1], fs.at[it])
         await_bytes(bsend.at[it, 0:(n_zone - 1) * CAP], bs.at[it])
-        await_bytes(rsend.at[it], rs.at[it])
+        for end in range(2):
+            await_bytes(rsend.at[it, end], rs.at[it, end])
         await_bytes(csend.at[it], cs.at[it])
         await_bytes(srecv.at[it, 0:devices - 1], ss.at[it])
         return 0
@@ -485,6 +558,7 @@
     landing = pltpu.VMEM((NEWTON, slots, 4, BLK), F32)
     blocks = SROWS * halves
     devices = n_vol * n_zone
+    wide = -(-rows * NNZ * 12 // BLK) * BLK
     dma = pltpu.SemaphoreType.DMA
     vmem = pl.BlockSpec(memory_space=pltpu.VMEM)
     hbm = pl.BlockSpec(memory_space=pltpu.HBM)
@@ -509,12 +583,13 @@
             field, field, field,
             pltpu.VMEM((halves, height, BLK), F32),
             pltpu.VMEM((KRY, comps, halves, SROWS, BLK), F32),
+            pltpu.VMEM((KRY, 4, 8, BLK), F32),
             pltpu.VMEM((KRY, rows * 8, BLK), F32),
             pltpu.VMEM((rows * 8, BLK), F32),
             pltpu.VMEM((rows, BLK, NNZ * BLK), BF16),
             pltpu.VMEM((rows, BLK, NNZ * BLK), BF16),
-            pltpu.VMEM((slots * 4, rows * NNZ * 8), BF16),
-            pltpu.VMEM((rows * NNZ * 8, BLK), F32),
+            pltpu.VMEM((slots * 4, wide), BF16),
+            pltpu.VMEM((wide, BLK), F32),
             pltpu.VMEM((blocks * 8, BLK), F32),
             pltpu.VMEM((blocks + 1, 8, BLK), F32),
             pltpu.VMEM((blocks * 8, BLK), F32),
@@ -531,7 +606,7 @@
             pltpu.VMEM((STEPS, 1, BLK), F32),
             pltpu.VMEM((STEPS, devices, 1, BLK), F32),
             dma((7,)),
-        ] + [dma((STEPS,))] * 10,
+        ] + [dma((STEPS,))] * 4 + [dma((STEPS, 2))] * 2 + [dma((STEPS,))] * 4,
         compiler_params=pltpu.CompilerParams(
             collective_id=0, has_side_effects=True, vmem_limit_bytes=32 * 1024 * 1024
         ),

time: 67.3 us -> 64.4 us (0.957)
  Pallas kernels: 65.1 us -> 62.2 us
    pallas_call x1, Pallas kernels: 65.1 us -> 62.2 us  [local(): pl.pallas_call(functools.partial(kernel, n_vol, n_zone), out_shape=[jax.S...]
where the time goes in v5:
time: 64.4 us; the launch traced here: 64.3 us
  Pallas kernels  62.2 us (97%)
  local copies, waits for them, and re-layouts  1.49 us (2%)
    pallas_call x1, Pallas kernels, local(): pl.pallas_call(functools.partial(kernel, n_vol, n_zone), out_shape=[jax.S...  62.2 us
    unnamed x2, local copies, waits for them, and re-layouts  1.49 us

profile of v5, /device:TPU:1, one launch (start us, length us, event | category | flops | bytes accessed | tf_op | source)
XLA Modules:
  0.0 64.3 jit_solution(8126758783017650597)
XLA Ops:
  0.6 62.2 %shard_map.86 = (f32[3,128,256]{2,1,0:T(8,128)S(1)}, f32[3,128,256]{2,1,0:T(8,128)S(1)}) custom-call(f32[3,128,256]{2,1,0:T(8,128)} %load_hbm.1, f32[128,256]{1,0:T(8,128)} %stiff_hbm.1, s32[2,128]{1,0:T(2,128)} %bitcast.3, s32[1,1,16]{2,1,0:T(1,128)} %owner_hbm.1, s32[1,3,1,16]{3,2,1,0:T(1,128)} %bitcast.2, s32[1,1,16]{2,1,0:T(1,128)} %active_hbm.1, ...), custom_call_target="tpu_custom_call" | custom-call | tf_op jit(solution)/shard_map/pallas_call | solution.py:568
  62.8 0.7 %copy.11 = f32[3,128,256]{2,1,0:T(8,128)} copy(f32[3,128,256]{2,1,0:T(8,128)S(1)} %get-tuple-element.4) | data formatting | bytes 786432
  63.6 0.7 %copy.12 = f32[3,128,256]{2,1,0:T(8,128)} copy(f32[3,128,256]{2,1,0:T(8,128)S(1)} %get-tuple-element.5) | data formatting | bytes 786432

commit v6 on v5

--- a/solution.py
+++ b/solution.py
@@ -34,7 +34,7 @@
     surf_ref, block_ref, back_ref,
     pack_tab, unpack_tab,
     fsend, frecv0, frecv1, frecv2, bsend, brecv0, brecv1, brecv2, rsend, rrecv, csend, crecv, ssend, srecv,
-    in_sem, fs, fr, bs, br, rs, rr, cs, cr, ss, sr,
+    here, in_sem, fs, fr, bs, br, rs, rr, cs, cr, ss, sr,
 ):
     frecv, brecv = (frecv0, frecv1, frecv2), (brecv0, brecv1, brecv2)
     comps, height = load_ref.shape[0], load_ref.shape[1]
@@ -70,8 +70,10 @@
     others.sort(key=lambda offset: -hops(offset))
 
     barrier = pltpu.get_barrier_semaphore()
-    for v, z in others:
-        pl.semaphore_signal(barrier, inc=1, device_id={"vol": at_vol(v), "zone": at_zone(z)})
+    for v in (10, 9, 11, 6, 14, 8, 2, 5, 7, 13, 15, 4, 12, 1, 3):
+        pl.semaphore_signal(barrier, inc=1, device_id={"vol": at_vol(v)})
+    for z in (4, 3, 5, 2, 6, 1, 7):
+        pl.semaphore_signal(barrier, inc=1, device_id={"zone": at_zone(z)})
 
     sub = lax.broadcasted_iota(jnp.int32, (8, BLK), 0)
     lane = lax.broadcasted_iota(jnp.int32, (8, BLK), 1)
@@ -146,7 +148,9 @@
         fetches[6].wait()
         lax.fori_loop(0, rows, split, 0)
 
-    pl.semaphore_wait(barrier, devices - 1)
+    pl.semaphore_wait(barrier, n_vol - 1 + n_zone - 1)
+    for v in range(1, n_vol):
+        pl.semaphore_signal(here, inc=1, device_id={"vol": at_vol(v)})
 
     def remote(src, dst, send, recv, target):
         return pltpu.make_async_remote_copy(
@@ -205,16 +209,19 @@
             rsend.at[it, end], rrecv.at[it, 1 - end], rs.at[it, end], rr.at[it, 1 - end], {"vol": target}
         ).start()
 
-    def send_strips(j, it):
+    def pack_strips(j, it, chosen, strips):
         for end, b, column in ((0, 0, 0), (1, halves - 1, BLK - 1)):
-            strip = zero
+            strip = strips(end)
             for c in range(comps):
-                for g in range(groups):
+                for g in chosen:
                     tile = x_ref[j, c, b, PAD + g * 8:PAD + g * 8 + 8, :]
                     strip = jnp.where(
                         lane == c * groups + g, jnp.broadcast_to(tile[:, column:column + 1], (8, BLK)), strip
                     )
             csend[it, end] = strip
+
+    def send_strips(j, it):
+        pack_strips(j, it, range(1), lambda end: csend[it, end])
         remote(csend.at[it, 0], crecv.at[it, 1], cs.at[it], cr.at[it], {"zone": at_zone(n_zone - 1)}).start()
         remote(csend.at[it, 1], crecv.at[it, 0], cs.at[it], cr.at[it], {"zone": at_zone(1)}).start()
 
@@ -371,7 +378,11 @@
 
     def finish_sums(it):
         await_bytes(srecv.at[it, 0:devices - 1], sr.at[it])
-        total = jnp.sum(srecv[it], axis=0)
+        total = srecv[it]
+        while total.shape[0] > 1:
+            half = total.shape[0] // 2
+            total = total[:half] + total[half:]
+        total = total[0]
         place = lane[0:1]
         return [
             jnp.sum(jnp.where(place // 32 == i, total, 0.0), axis=1, keepdims=True) for i in range(3)
@@ -396,24 +407,30 @@
         it = n * KRY
 
         inner(0)
+
+        def dots0(c, b, padded, at, sums):
+            x = x_ref[0, c, b, padded, :]
+            q = l_ref[0, c, b, at, :] + d_ref[c, b, at, :] * x
+            return sums[0] + x * x, sums[1] + x * q
+
+        gamma, delta = over_tiles(dots0, (zero, zero))
         find_gaps(0, n)
         push_forces(0, n)
         take_row(0, it, 0)
         take_strips(0, it)
+        delta = delta + energy(lambda at: gap_ref[0, at, :]) - edges(lambda part: part(0, it))
+
+        @pl.when(n == 0)
+        def _():
+            pl.semaphore_wait(here, n_vol - 1)
+
+        start_sums(it, gamma, delta, zero)
         first_rows(0)
         send_surface(1, n)
-
-        def dots0(c, b, padded, at, sums):
-            x = x_ref[0, c, b, padded, :]
-            q = l_ref[0, c, b, at, :] + d_ref[c, b, at, :] * x
-            return sums[0] + x * x, sums[1] + x * q
-
-        gamma, delta = over_tiles(dots0, (zero, zero))
-        delta = delta + energy(lambda at: gap_ref[0, at, :]) - edges(lambda part: part(0, it))
-        start_sums(it, gamma, delta, zero)
         take_row(0, it, 1)
         other_rows(0)
         send_row(1, it + 1, 1)
+        pack_strips(1, it + 1, range(1, groups), lambda end: zero)
         receive_forces(0, n)
         add_contact(0)
         send_strips(1, it + 1)
@@ -443,6 +460,7 @@
         take_row(1, it + 1, 1)
         other_rows(1)
         send_row(2, it + 2, 1)
+        pack_strips(2, it + 2, range(1, groups), lambda end: zero)
         receive_forces(1, n)
         add_contact(1)
         send_strips(2, it + 2)
@@ -519,7 +537,13 @@
 
         apply_row(lu_ref, 0, 1, under)
         apply_strips(lu_ref, 0, left, right, range(1, groups))
-        lax.fori_loop(1, groups, finish, 0)
+        finish(groups - 1, 0)
+
+        @pl.when(n < NEWTON - 1)
+        def _():
+            send_row(0, it + KRY, 1)
+
+        lax.fori_loop(1, groups - 1, finish, 0)
 
         @pl.when(n < NEWTON - 1)
         def _():
@@ -528,10 +552,11 @@
         return 0
 
     def send_outline(it):
-        send_row(0, it, 1)
+        pack_strips(0, it, range(1, groups), lambda end: zero)
+        send_strips(0, it)
         send_row(0, it, 0)
-        send_strips(0, it)
-
+
+    send_row(0, 0, 1)
     send_surface(0, 0)
     send_outline(0)
     set_up()
@@ -605,6 +630,7 @@
             pltpu.VMEM((STEPS, 2, 8, BLK), F32),
             pltpu.VMEM((STEPS, 1, BLK), F32),
             pltpu.VMEM((STEPS, devices, 1, BLK), F32),
+            pltpu.SemaphoreType.REGULAR,
             dma((7,)),
         ] + [dma((STEPS,))] * 4 + [dma((STEPS, 2))] * 2 + [dma((STEPS,))] * 4,
         compiler_params=pltpu.CompilerParams(

time: 64.4 us -> 62.9 us (0.977)
  Pallas kernels: 62.2 us -> 60.6 us
    pallas_call x1, Pallas kernels: 62.2 us -> 60.6 us  [local(): pl.pallas_call(functools.partial(kernel, n_vol, n_zone), out_shape=[jax.S...]
where the time goes in v6:
time: 62.9 us; the launch traced here: 62.8 us
  Pallas kernels  60.6 us (96%)
  local copies, waits for them, and re-layouts  1.49 us (2%)
  between operations  0.64 us (1%)
    pallas_call x1, Pallas kernels, local(): pl.pallas_call(functools.partial(kernel, n_vol, n_zone), out_shape=[jax.S...  60.6 us
    unnamed x2, local copies, waits for them, and re-layouts  1.49 us

profile of v6, /device:TPU:1, one launch (start us, length us, event | category | flops | bytes accessed | tf_op | source)
XLA Modules:
  0.0 62.8 jit_solution(5810599667675050271)
XLA Ops:
  0.6 60.6 %shard_map.86 = (f32[3,128,256]{2,1,0:T(8,128)S(1)}, f32[3,128,256]{2,1,0:T(8,128)S(1)}) custom-call(f32[3,128,256]{2,1,0:T(8,128)} %load_hbm.1, f32[128,256]{1,0:T(8,128)} %stiff_hbm.1, s32[2,128]{1,0:T(2,128)} %bitcast.3, s32[1,1,16]{2,1,0:T(1,128)} %owner_hbm.1, s32[1,3,1,16]{3,2,1,0:T(1,128)} %bitcast.2, s32[1,1,16]{2,1,0:T(1,128)} %active_hbm.1, ...), custom_call_target="tpu_custom_call" | custom-call | tf_op jit(solution)/shard_map/pallas_call | solution.py:593
  61.3 0.7 %copy.11 = f32[3,128,256]{2,1,0:T(8,128)} copy(f32[3,128,256]{2,1,0:T(8,128)S(1)} %get-tuple-element.4) | data formatting | bytes 786432
  62.0 0.7 %copy.12 = f32[3,128,256]{2,1,0:T(8,128)} copy(f32[3,128,256]{2,1,0:T(8,128)S(1)} %get-tuple-element.5) | data formatting | bytes 786432

commit v7 on v6

--- a/solution.py
+++ b/solution.py
@@ -29,11 +29,11 @@
     load_hbm, stiff_hbm, flags_hbm, owner_hbm, pattern_hbm, active_hbm, mortar_ref,
     u_ref, res_ref,
     load_ref, stiff_ref, flags_ref, owner_ref, pattern_ref, active_ref, mort_ref,
-    x_ref, l_ref, r_ref, d_ref, lu_ref, hard_ref, contact_ref, halo_ref, gap_ref, scale_ref,
+    x_ref, l_ref, r_ref, d_ref, lu_ref, hard_ref, contact_ref, halo_ref, own_ref, slot_ref, coef_ref, gap_ref, scale_ref,
     mhi_ref, mlo_ref, spread_ref, push_ref,
     surf_ref, block_ref, back_ref,
     pack_tab, unpack_tab,
-    fsend, frecv0, frecv1, frecv2, bsend, brecv0, brecv1, brecv2, rsend, rrecv, csend, crecv, ssend, srecv,
+    fsend, frecv0, frecv1, frecv2, fixed, bsend, brecv0, brecv1, brecv2, rsend, rrecv, csend, crecv, ssend, srecv,
     here, in_sem, fs, fr, bs, br, rs, rr, cs, cr, ss, sr,
 ):
     frecv, brecv = (frecv0, frecv1, frecv2), (brecv0, brecv1, brecv2)
@@ -109,7 +109,7 @@
         fetch.wait()
     for c in range(comps):
         for b in range(halves):
-            for j in range(KRY):
+            for j in range(KRY + 1):
                 x_ref[j, c, b, 0:PAD, :] = jnp.zeros((PAD, BLK), F32)
                 x_ref[j, c, b, PAD + height:, :] = jnp.zeros((PAD, BLK), F32)
             x_ref[0, c, b, PAD:PAD + height, :] = load_ref[c, :, b * BLK:(b + 1) * BLK]
@@ -178,11 +178,10 @@
 
         return lax.fori_loop(0, groups, group, init, unroll=2)
 
-    def send_surface(j, n):
-        it = n * KRY + j
+    def send_surface(it, tile, landing):
         for c in range(comps):
             for b in range(halves):
-                surf_ref[pl.ds(b * 8 + c, SROWS, stride=8 * halves), :] = x_ref[j, c, b, PAD:PAD + SROWS, :]
+                surf_ref[pl.ds(b * 8 + c, SROWS, stride=8 * halves), :] = tile(c, b)
         for m in range(blocks):
             block_ref[m] = surf_ref[m * 8:m * 8 + 8, :]
         for step in (4, 3, 5, 2, 6, 1, 7, 0):
@@ -192,11 +191,12 @@
                 if step:
                     fsend[it, step, k] = block
                 else:
-                    frecv[j][n, zone * CAP + k] = block
+                    landing[zone * CAP + k] = block
             if step:
-                remote(
-                    fsend.at[it, step], frecv[j].at[n, slots_of(zone)], fs.at[it], fr.at[it], {"zone": z}
-                ).start()
+                remote(fsend.at[it, step], landing.at[slots_of(zone)], fs.at[it], fr.at[it], {"zone": z}).start()
+
+    def send_field(j, it, landing):
+        send_surface(it, lambda c, b: x_ref[j, c, b, PAD:PAD + SROWS, :], landing)
 
     def send_row(j, it, end):
         at = PAD + (height - 1 if end else 0)
@@ -204,24 +204,36 @@
             for b in range(halves):
                 i = c * halves + b
                 rsend[it, end, i:i + 1, :] = x_ref[j, c, b, at:at + 1, :]
+        if end == 0:
+            own_ref[j, 0] = rsend[it, 0]
+        ship_row(it, end)
+
+    def ship_row(it, end):
         target = at_vol(1 if end else n_vol - 1)
         remote(
             rsend.at[it, end], rrecv.at[it, 1 - end], rs.at[it, end], rr.at[it, 1 - end], {"vol": target}
         ).start()
 
+    def strip_of(field, end, chosen, strip):
+        b, column = (halves - 1, BLK - 1) if end else (0, 0)
+        for c in range(comps):
+            for g in chosen:
+                tile = field[c, b, PAD + g * 8:PAD + g * 8 + 8, :]
+                strip = jnp.where(
+                    lane == c * groups + g, jnp.broadcast_to(tile[:, column:column + 1], (8, BLK)), strip
+                )
+        return strip
+
     def pack_strips(j, it, chosen, strips):
-        for end, b, column in ((0, 0, 0), (1, halves - 1, BLK - 1)):
-            strip = strips(end)
-            for c in range(comps):
-                for g in chosen:
-                    tile = x_ref[j, c, b, PAD + g * 8:PAD + g * 8 + 8, :]
-                    strip = jnp.where(
-                        lane == c * groups + g, jnp.broadcast_to(tile[:, column:column + 1], (8, BLK)), strip
-                    )
-            csend[it, end] = strip
+        for end in range(2):
+            csend[it, end] = strip_of(x_ref.at[j], end, chosen, strips(end))
 
     def send_strips(j, it):
         pack_strips(j, it, range(1), lambda end: csend[it, end])
+        own_ref[j, 1] = csend[it, 0]
+        ship_strips(it)
+
+    def ship_strips(it):
         remote(csend.at[it, 0], crecv.at[it, 1], cs.at[it], cr.at[it], {"zone": at_zone(n_zone - 1)}).start()
         remote(csend.at[it, 1], crecv.at[it, 0], cs.at[it], cr.at[it], {"zone": at_zone(1)}).start()
 
@@ -269,11 +281,15 @@
 
         lax.fori_loop(0, groups, group, 0, unroll=2)
 
+    def image(j, c, b, at, padded):
+        part = l_ref[j, c, b, at, :]
+        return part + d_ref[c, b, at, :] * x_ref[j, c, b, padded, :] if j < KRY - 1 else part
+
     def first_rows(j):
         for c in range(comps):
             for b in range(halves):
                 at = slice(PAD, PAD + SROWS)
-                x_ref[j + 1, c, b, at, :] = l_ref[j, c, b, 0:SROWS, :] + d_ref[c, b, 0:SROWS, :] * x_ref[j, c, b, at, :]
+                x_ref[j + 1, c, b, at, :] = image(j, c, b, slice(0, SROWS), at)
         field = x_ref.at[j + 1]
         apply_row(field, PAD, 0, halo_ref[j, 0])
         apply_strips(field, PAD, halo_ref[j, 2], halo_ref[j, 3], range(1))
@@ -282,10 +298,7 @@
         def group(g, _):
             for c in range(comps):
                 for b in range(halves):
-                    x = x_ref[j, c, b, group_rows(g), :]
-                    x_ref[j + 1, c, b, group_rows(g), :] = (
-                        l_ref[j, c, b, tile_rows(g), :] + d_ref[c, b, tile_rows(g), :] * x
-                    )
+                    x_ref[j + 1, c, b, group_rows(g), :] = image(j, c, b, tile_rows(g), group_rows(g))
             return 0
 
         lax.fori_loop(1, groups, group, 0, unroll=3)
@@ -306,14 +319,14 @@
         product = product[0:8] + product[8:16]
         return product + pltpu.roll(product, 4, axis=0)
 
-    def find_gaps(j, n):
+    def fill_slots(j, n):
         it = n * KRY + j
         await_bytes(frecv[j].at[n, 0:(n_zone - 1) * CAP], fr.at[it])
+        slot_ref[j] = frecv[j][n] + bsend[it - 1] if j else frecv[j][n]
+
+    def find_gaps(j):
         for r in range(rows):
-            picked = jnp.concatenate([frecv[j][n, link(r, k)] for k in range(NNZ)], axis=1)
-            if j:
-                picked = picked + jnp.concatenate([bsend[it - 1, link(r, k)] for k in range(NNZ)], axis=1)
-            picked = split_rows(picked)
+            picked = split_rows(jnp.concatenate([slot_ref[j, link(r, k)] for k in range(NNZ)], axis=1))
             gap = lax.dot_general(picked, mhi_ref[r], contract_last, preferred_element_type=F32)
             gap = gap + lax.dot_general(picked, mlo_ref[r], contract_last, preferred_element_type=F32)
             gap_ref[j, r * 8:r * 8 + 8, :] = join_rows(gap)
@@ -399,8 +412,8 @@
 
     def edges(mix):
         return 2.0 * (
-            mix(lambda j, it: rsend[it + j, 0]) * mix(lambda j, it: halo_ref[j, 0])
-            + mix(lambda j, it: csend[it + j, 0]) * mix(lambda j, it: halo_ref[j, 2])
+            mix(lambda j: own_ref[j, 0]) * mix(lambda j: halo_ref[j, 0])
+            + mix(lambda j: own_ref[j, 1]) * mix(lambda j: halo_ref[j, 2])
         )
 
     def newton(n, _):
@@ -414,11 +427,16 @@
             return sums[0] + x * x, sums[1] + x * q
 
         gamma, delta = over_tiles(dots0, (zero, zero))
-        find_gaps(0, n)
-        push_forces(0, n)
-        take_row(0, it, 0)
-        take_strips(0, it)
-        delta = delta + energy(lambda at: gap_ref[0, at, :]) - edges(lambda part: part(0, it))
+
+        @pl.when(n == 0)
+        def _():
+            fill_slots(0, 0)
+            find_gaps(0)
+            push_forces(0, 0)
+            take_row(0, 0, 0)
+            take_strips(0, 0)
+
+        delta = delta + energy(lambda at: gap_ref[0, at, :]) - edges(lambda part: part(0))
 
         @pl.when(n == 0)
         def _():
@@ -426,8 +444,17 @@
 
         start_sums(it, gamma, delta, zero)
         first_rows(0)
-        send_surface(1, n)
-        take_row(0, it, 1)
+        send_field(1, it + 1, frecv[1].at[n])
+
+        @pl.when(n == 0)
+        def _():
+            take_row(0, 0, 1)
+
+        @pl.when(n > 0)
+        def _():
+            take_row(KRY, KRY, 1)
+            derive_halo(1)
+
         other_rows(0)
         send_row(1, it + 1, 1)
         pack_strips(1, it + 1, range(1, groups), lambda end: zero)
@@ -436,14 +463,15 @@
         send_strips(1, it + 1)
         send_row(1, it + 1, 0)
         inner(1)
-        find_gaps(1, n)
+        fill_slots(1, n)
+        find_gaps(1)
         push_forces(1, n)
         gamma0, pq0, _ = finish_sums(it)
         a0 = gamma0 / pq0
         take_row(1, it + 1, 0)
         take_strips(1, it + 1)
         first_rows(1)
-        send_surface(2, n)
+        send_field(2, it + 2, frecv[2].at[n])
         w0 = full(a0)
 
         def dots1(c, b, padded, at, sums):
@@ -455,7 +483,7 @@
 
         gamma, delta, cross = over_tiles(dots1, (zero, zero, zero))
         delta = delta + energy(lambda at: gap_ref[0, at, :] - w0 * gap_ref[1, at, :])
-        delta = delta - edges(lambda part: part(0, it) - w0 * part(1, it))
+        delta = delta - edges(lambda part: part(0) - w0 * part(1))
         start_sums(it + 1, gamma, delta, cross)
         take_row(1, it + 1, 1)
         other_rows(1)
@@ -466,7 +494,9 @@
         send_strips(2, it + 2)
         send_row(2, it + 2, 0)
         inner(2)
-        find_gaps(2, n)
+        fill_slots(2, n)
+        find_gaps(2)
+        push_forces(2, n)
         gamma1, delta, cross = finish_sums(it + 1)
         beta1 = gamma1 / gamma0
         pq1 = delta + beta1 * (2.0 * cross + beta1 * pq0)
@@ -487,11 +517,30 @@
 
         gamma, delta, cross = over_tiles(dots2, (zero, zero, zero))
         delta = delta + energy(lambda at: second(gap_ref[0, at, :], gap_ref[1, at, :], gap_ref[2, at, :]))
-        delta = delta - edges(lambda part: second(part(0, it), part(1, it), part(2, it)))
+        delta = delta - edges(lambda part: second(part(0), part(1), part(2)))
         start_sums(it + 2, gamma, delta, cross)
-        push_forces(2, n)
+
+        @pl.when(n < NEWTON - 1)
+        def _():
+            first_rows(2)
+            send_field(KRY, KRY, frecv[0].at[1])
+
         take_row(2, it + 2, 1)
+
+        @pl.when(n < NEWTON - 1)
+        def _():
+            other_rows(2)
+            send_row(KRY, KRY, 1)
+            pack_strips(KRY, KRY, range(1, groups), lambda end: zero)
+
         receive_forces(2, n)
+
+        @pl.when(n < NEWTON - 1)
+        def _():
+            add_contact(2)
+            send_strips(KRY, KRY)
+            send_row(KRY, KRY, 0)
+
         gamma2, delta, cross = finish_sums(it + 2)
         beta2 = gamma2 / gamma1
         pq2 = delta + beta2 * (2.0 * cross + beta2 * pq1)
@@ -500,6 +549,14 @@
         k0 = full(a0 + a1 * (1.0 + beta1) + a2 * (1.0 + turned))
         k1 = full(-(a1 * a0 + a2 * (a0 + a1 * (1.0 + beta1) + beta2 * a0)))
         k2 = full(a2 * a1 * a0)
+
+        coef_ref[0], coef_ref[1], coef_ref[2] = k0, k1, k2
+
+        @pl.when(n < NEWTON - 1)
+        def _():
+            derive_slots()
+            find_gaps(0)
+            push_forces(0, 1)
 
         def mix(fields):
             return k0 * fields(0) + k1 * fields(1) + k2 * fields(2)
@@ -530,48 +587,112 @@
             return 0
 
         finish(0, 0)
-
-        @pl.when(n < NEWTON - 1)
-        def _():
-            send_surface(0, n + 1)
-
         apply_row(lu_ref, 0, 1, under)
         apply_strips(lu_ref, 0, left, right, range(1, groups))
-        finish(groups - 1, 0)
+        lax.fori_loop(1, groups, finish, 0)
 
         @pl.when(n < NEWTON - 1)
         def _():
-            send_row(0, it + KRY, 1)
-
-        lax.fori_loop(1, groups - 1, finish, 0)
-
-        @pl.when(n < NEWTON - 1)
-        def _():
-            send_outline(it + KRY)
+            for c in range(comps):
+                for b in range(halves):
+                    i = c * halves + b
+                    own_ref[0, 0, i:i + 1, :] = x_ref[0, c, b, PAD:PAD + 1, :]
+            own_ref[0, 1] = strip_of(x_ref.at[0], 0, range(groups), zero)
+            take_row(KRY, KRY, 0)
+            take_strips(KRY, KRY)
+            await_bytes(crecv.at[STEPS], cr.at[STEPS])
+            for i in (0, 2, 3):
+                derive_halo(i)
 
         return 0
 
-    def send_outline(it):
-        pack_strips(0, it, range(1, groups), lambda end: zero)
-        send_strips(0, it)
-        send_row(0, it, 0)
-
+    def next_residual(loads, stiff, hard, first, second, third, last):
+        k0, k1, k2 = [coef_ref[j] for j in range(KRY)]
+        if len(first.shape) == 3:
+            k0, k1, k2 = k0[0:4][None], k1[0:4][None], k2[0:4][None]
+        u = k0 * first + k1 * second + k2 * third
+        moved = k0 * (second - stiff * first) + k1 * (third - stiff * second) + k2 * last
+        material = stiff * (hard * u + (1.0 - hard) * yield_scale * jnp.tanh(u / yield_scale))
+        return loads - (moved + material)
+
+    def derive_slots():
+        await_bytes(fixed.at[0:(n_zone - 1) * CAP], fr.at[STEPS])
+        await_bytes(frecv[0].at[1, 0:(n_zone - 1) * CAP], fr.at[KRY])
+        stiff = jnp.broadcast_to(fixed[:, 0:1, :], fixed.shape)
+        hard = jnp.broadcast_to(fixed[:, 1:2, :], fixed.shape)
+        fields = [slot_ref[j] for j in range(KRY)]
+        slot_ref[0] = next_residual(fields[0], stiff, hard, *fields, frecv[0][1] + bsend[KRY - 1])
+
+    def derive_halo(i):
+        if i < 2:
+            await_bytes(rrecv.at[STEPS, i], rr.at[STEPS, i])
+            packed = rrecv[STEPS, i]
+            stiff, hard = [
+                jnp.where(
+                    sub < comps * halves,
+                    jnp.where(lax.rem(sub, halves) == 0, packed[e:e + 1], packed[e + 1:e + 2]), 0.0,
+                )
+                for e in (0, halves)
+            ]
+        else:
+            packed = crecv[STEPS, i - 2]
+            parts = [
+                jnp.where(lane < groups, packed, 0.0),
+                jnp.where(lane < groups, pltpu.roll(packed, BLK - groups, axis=1), 0.0),
+            ]
+            stiff, hard = [
+                part + pltpu.roll(part, groups, axis=1) + pltpu.roll(part, 2 * groups, axis=1) for part in parts
+            ]
+        fields = [halo_ref[j, i] for j in range(KRY + 1)]
+        halo_ref[0, i] = next_residual(fields[0], stiff, hard, *fields)
+
+    def send_fixed():
+        def tile(c, b):
+            if c == 0:
+                return stiff_ref[0:SROWS, b * BLK:(b + 1) * BLK]
+            return hard_ref[b, 0:SROWS, :] if c == 1 else zero
+
+        send_surface(STEPS, tile, fixed)
+        for end, at in ((0, 0), (1, height - 1)):
+            for b in range(halves):
+                rsend[STEPS, end, b:b + 1, :] = stiff_ref[at:at + 1, b * BLK:(b + 1) * BLK]
+                rsend[STEPS, end, halves + b:halves + b + 1, :] = hard_ref[b, at:at + 1, :]
+            ship_row(STEPS, end)
+        for end, b, column in ((0, 0, 0), (1, halves - 1, BLK - 1)):
+            strip = zero
+            for g in range(groups):
+                at = slice(g * 8, g * 8 + 8)
+                for e, tile8 in ((0, stiff_ref[at, b * BLK:(b + 1) * BLK]), (groups, hard_ref[b, at, :])):
+                    strip = jnp.where(
+                        lane == e + g, jnp.broadcast_to(tile8[:, column:column + 1], (8, BLK)), strip
+                    )
+            csend[STEPS, end] = strip
+        ship_strips(STEPS)
+
+    own_ref[0, 0] = zero
     send_row(0, 0, 1)
-    send_surface(0, 0)
-    send_outline(0)
+    send_field(0, 0, frecv[0].at[0])
+    pack_strips(0, 0, range(1, groups), lambda end: zero)
+    send_strips(0, 0)
+    send_row(0, 0, 0)
     set_up()
+    send_fixed()
     lax.fori_loop(0, NEWTON, newton, 0)
 
     def drain(it, _):
         await_bytes(fsend.at[it, 0:n_zone - 1], fs.at[it])
-        await_bytes(bsend.at[it, 0:(n_zone - 1) * CAP], bs.at[it])
         for end in range(2):
             await_bytes(rsend.at[it, end], rs.at[it, end])
         await_bytes(csend.at[it], cs.at[it])
+        return 0
+
+    def drain_sums(it, _):
+        await_bytes(bsend.at[it, 0:(n_zone - 1) * CAP], bs.at[it])
         await_bytes(srecv.at[it, 0:devices - 1], ss.at[it])
         return 0
 
-    lax.fori_loop(0, STEPS, drain, 0)
+    lax.fori_loop(0, STEPS + 1, drain, 0)
+    lax.fori_loop(0, STEPS, drain_sums, 0)
 
 
 def local(n_vol, n_zone, load, support_stiffness, plastic_flags, owner_map, pattern, active, mortar):
@@ -603,12 +724,15 @@
             pltpu.SMEM(links.shape, jnp.int32),
             pltpu.SMEM(active.shape, jnp.int32),
             pltpu.VMEM(mortar.shape[2:], F32),
-            pltpu.VMEM((KRY, comps, halves, height + 2 * PAD, BLK), F32),
+            pltpu.VMEM((KRY + 1, comps, halves, height + 2 * PAD, BLK), F32),
             pltpu.VMEM((KRY, comps, halves, height, BLK), F32),
             field, field, field,
             pltpu.VMEM((halves, height, BLK), F32),
             pltpu.VMEM((KRY, comps, halves, SROWS, BLK), F32),
-            pltpu.VMEM((KRY, 4, 8, BLK), F32),
+            pltpu.VMEM((KRY + 1, 4, 8, BLK), F32),
+            pltpu.VMEM((KRY + 1, 2, 8, BLK), F32),
+            pltpu.VMEM((KRY, slots, 4, BLK), F32),
+            pltpu.VMEM((KRY, 8, BLK), F32),
             pltpu.VMEM((KRY, rows * 8, BLK), F32),
             pltpu.VMEM((rows * 8, BLK), F32),
             pltpu.VMEM((rows, BLK, NNZ * BLK), BF16),
@@ -620,19 +744,20 @@
             pltpu.VMEM((blocks * 8, BLK), F32),
             pltpu.SMEM((slots,), jnp.int32),
             pltpu.SMEM((blocks,), jnp.int32),
-            pltpu.VMEM((STEPS, n_zone, CAP, 4, BLK), F32),
+            pltpu.VMEM((STEPS + 1, n_zone, CAP, 4, BLK), F32),
             landing, landing, landing,
+            pltpu.VMEM((slots, 4, BLK), F32),
             pltpu.VMEM((STEPS, slots, 4, BLK), F32),
             landing, landing, landing,
-            pltpu.VMEM((STEPS, 2, 8, BLK), F32),
-            pltpu.VMEM((STEPS, 2, 8, BLK), F32),
-            pltpu.VMEM((STEPS, 2, 8, BLK), F32),
-            pltpu.VMEM((STEPS, 2, 8, BLK), F32),
+            pltpu.VMEM((STEPS + 1, 2, 8, BLK), F32),
+            pltpu.VMEM((STEPS + 1, 2, 8, BLK), F32),
+            pltpu.VMEM((STEPS + 1, 2, 8, BLK), F32),
+            pltpu.VMEM((STEPS + 1, 2, 8, BLK), F32),
             pltpu.VMEM((STEPS, 1, BLK), F32),
             pltpu.VMEM((STEPS, devices, 1, BLK), F32),
             pltpu.SemaphoreType.REGULAR,
             dma((7,)),
-        ] + [dma((STEPS,))] * 4 + [dma((STEPS, 2))] * 2 + [dma((STEPS,))] * 4,
+        ] + [dma((STEPS + 1,))] * 4 + [dma((STEPS + 1, 2))] * 2 + [dma((STEPS + 1,))] * 4,
         compiler_params=pltpu.CompilerParams(
             collective_id=0, has_side_effects=True, vmem_limit_bytes=32 * 1024 * 1024
         ),

time: 62.9 us -> 62.1 us (0.987)
  Pallas kernels: 60.6 us -> 59.8 us
    pallas_call x1, Pallas kernels: 60.6 us -> 59.8 us  [local(): pl.pallas_call(functools.partial(kernel, n_vol, n_zone), out_shape=[jax.S...]
where the time goes in v7:
time: 62.1 us; the launch traced here: 62 us
  Pallas kernels  59.8 us (96%)
  local copies, waits for them, and re-layouts  1.49 us (2%)
  between operations  0.64 us (1%)
    pallas_call x1, Pallas kernels, local(): pl.pallas_call(functools.partial(kernel, n_vol, n_zone), out_shape=[jax.S...  59.8 us
    unnamed x2, local copies, waits for them, and re-layouts  1.49 us

profile of v7, /device:TPU:1, one launch (start us, length us, event | category | flops | bytes accessed | tf_op | source)
XLA Modules:
  0.0 62.0 jit_solution(17548624088407805026)
XLA Ops:
  0.6 59.8 %shard_map.86 = (f32[3,128,256]{2,1,0:T(8,128)S(1)}, f32[3,128,256]{2,1,0:T(8,128)S(1)}) custom-call(f32[3,128,256]{2,1,0:T(8,128)} %load_hbm.1, f32[128,256]{1,0:T(8,128)} %stiff_hbm.1, s32[2,128]{1,0:T(2,128)} %bitcast.3, s32[1,1,16]{2,1,0:T(1,128)} %owner_hbm.1, s32[1,3,1,16]{3,2,1,0:T(1,128)} %bitcast.2, s32[1,1,16]{2,1,0:T(1,128)} %active_hbm.1, ...), custom_call_target="tpu_custom_call" | custom-call | tf_op jit(solution)/shard_map/pallas_call | solution.py:714
  60.5 0.7 %copy.11 = f32[3,128,256]{2,1,0:T(8,128)} copy(f32[3,128,256]{2,1,0:T(8,128)S(1)} %get-tuple-element.4) | data formatting | bytes 786432
  61.2 0.7 %copy.12 = f32[3,128,256]{2,1,0:T(8,128)} copy(f32[3,128,256]{2,1,0:T(8,128)S(1)} %get-tuple-element.5) | data formatting | bytes 786432

commit v8 on v7

--- a/solution.py
+++ b/solution.py
@@ -169,14 +169,23 @@
     def tile_rows(g):
         return pl.ds(pl.multiple_of(g * 8, 8), 8)
 
-    def over_tiles(body, init):
-        def group(g, carry):
+    def sum_tiles(body, count):
+        def group(g, sums):
+            added = []
             for c in range(comps):
                 for b in range(halves):
-                    carry = body(c, b, group_rows(g), tile_rows(g), carry)
-            return carry
-
-        return lax.fori_loop(0, groups, group, init, unroll=2)
+                    terms = body(c, b, group_rows(g), tile_rows(g))
+                    added += [total + term for total, term in zip(sums[c * halves + b], terms)]
+            return tuple(tuple(added[i:i + count]) for i in range(0, len(added), count))
+
+        start = tuple(tuple(zero for _ in range(count)) for _ in range(comps * halves))
+        sums = lax.fori_loop(0, groups, group, start, unroll=4)
+        return [total_of([tile[i] for tile in sums]) for i in range(count)]
+
+    def total_of(terms):
+        while len(terms) > 1:
+            terms = [sum(terms[i:i + 2][1:], terms[i]) for i in range(0, len(terms), 2)]
+        return terms[0]
 
     def send_surface(it, tile, landing):
         for c in range(comps):
@@ -263,23 +272,32 @@
                     image = field[c, b, at, :]
                     field[c, b, at, :] = jnp.where(lane == column, image - spread, image)
 
-    def inner(j):
-        def group(g, _):
+    def inner(j, sums=False):
+        def group(g, totals):
+            totals = list(totals)
             for c in range(comps):
                 tiles = [x_ref[j, c, b, group_rows(g), :] for b in range(halves)]
                 to_right = [pltpu.roll(tile, 1, axis=1) for tile in tiles]
                 to_left = [pltpu.roll(tile, BLK - 1, axis=1) for tile in tiles]
                 for b in range(halves):
+                    x = tiles[b]
                     before = to_right[b - 1] if b > 0 else zero
                     after = to_left[b + 1] if b < halves - 1 else zero
                     left = jnp.where(lane == 0, before, to_right[b])
                     right = jnp.where(lane == BLK - 1, after, to_left[b])
                     over = x_ref[j, c, b, pl.ds(PAD + g * 8 - 1, 8), :]
                     under = x_ref[j, c, b, pl.ds(PAD + g * 8 + 1, 8), :]
-                    l_ref[j, c, b, tile_rows(g), :] = 4.0 * tiles[b] - (over + under + left + right)
-            return 0
-
-        lax.fori_loop(0, groups, group, 0, unroll=2)
+                    part = 4.0 * x - ((over + under) + (left + right))
+                    l_ref[j, c, b, tile_rows(g), :] = part
+                    if sums:
+                        i = 2 * (c * halves + b)
+                        totals[i] = totals[i] + x * x
+                        totals[i + 1] = totals[i + 1] + x * (part + d_ref[c, b, tile_rows(g), :] * x)
+            return tuple(totals)
+
+        start = (zero,) * (2 * comps * halves if sums else 0)
+        totals = lax.fori_loop(0, groups, group, start, unroll=4)
+        return [total_of(list(totals[i::2])) for i in range(2)] if sums else None
 
     def image(j, c, b, at, padded):
         part = l_ref[j, c, b, at, :]
@@ -301,7 +319,7 @@
                     x_ref[j + 1, c, b, group_rows(g), :] = image(j, c, b, tile_rows(g), group_rows(g))
             return 0
 
-        lax.fori_loop(1, groups, group, 0, unroll=3)
+        lax.fori_loop(1, groups, group, 0, unroll=5)
         field = x_ref.at[j + 1]
         apply_row(field, PAD, 1, halo_ref[j, 1])
         apply_strips(field, PAD, halo_ref[j, 2], halo_ref[j, 3], range(1, groups))
@@ -368,12 +386,12 @@
                 contact_ref[j, c, b] = back_ref[pl.ds(b * 8 + c, SROWS, stride=8 * halves), :]
 
     def energy(gaps):
-        total = zero
+        terms = []
         for r in range(rows):
             at = slice(r * 8, r * 8 + 8)
             gap = gaps(at)
-            total = total + scale_ref[at, :] * (gap * gap)
-        return 0.5 * total
+            terms.append(scale_ref[at, :] * (gap * gap))
+        return 0.5 * total_of(terms)
 
     def start_sums(it, gamma, delta, cross):
         parts = []
@@ -419,14 +437,7 @@
     def newton(n, _):
         it = n * KRY
 
-        inner(0)
-
-        def dots0(c, b, padded, at, sums):
-            x = x_ref[0, c, b, padded, :]
-            q = l_ref[0, c, b, at, :] + d_ref[c, b, at, :] * x
-            return sums[0] + x * x, sums[1] + x * q
-
-        gamma, delta = over_tiles(dots0, (zero, zero))
+        gamma, delta = inner(0, sums=True)
 
         @pl.when(n == 0)
         def _():
@@ -436,15 +447,15 @@
             take_row(0, 0, 0)
             take_strips(0, 0)
 
-        delta = delta + energy(lambda at: gap_ref[0, at, :]) - edges(lambda part: part(0))
 
         @pl.when(n == 0)
         def _():
             pl.semaphore_wait(here, n_vol - 1)
 
-        start_sums(it, gamma, delta, zero)
         first_rows(0)
         send_field(1, it + 1, frecv[1].at[n])
+        delta = delta + energy(lambda at: gap_ref[0, at, :]) - edges(lambda part: part(0))
+        start_sums(it, gamma, delta, zero)
 
         @pl.when(n == 0)
         def _():
@@ -466,22 +477,22 @@
         fill_slots(1, n)
         find_gaps(1)
         push_forces(1, n)
-        gamma0, pq0, _ = finish_sums(it)
-        a0 = gamma0 / pq0
         take_row(1, it + 1, 0)
         take_strips(1, it + 1)
         first_rows(1)
         send_field(2, it + 2, frecv[2].at[n])
+        gamma0, pq0, _ = finish_sums(it)
+        a0 = gamma0 / pq0
         w0 = full(a0)
 
-        def dots1(c, b, padded, at, sums):
+        def dots1(c, b, padded, at):
             x1 = x_ref[1, c, b, padded, :]
             r = x_ref[0, c, b, padded, :] - w0 * x1
             r_ref[c, b, at, :] = r
             q = (l_ref[0, c, b, at, :] - w0 * l_ref[1, c, b, at, :]) + d_ref[c, b, at, :] * r
-            return sums[0] + r * r, sums[1] + r * q, sums[2] + r * x1
-
-        gamma, delta, cross = over_tiles(dots1, (zero, zero, zero))
+            return r * r, r * q, r * x1
+
+        gamma, delta, cross = sum_tiles(dots1, 3)
         delta = delta + energy(lambda at: gap_ref[0, at, :] - w0 * gap_ref[1, at, :])
         delta = delta - edges(lambda part: part(0) - w0 * part(1))
         start_sums(it + 1, gamma, delta, cross)
@@ -508,14 +519,14 @@
         def second(x0, x1, x2):
             return (x0 - w0 * x1) - w1 * (more * x1 - w0 * x2)
 
-        def dots2(c, b, padded, at, sums):
+        def dots2(c, b, padded, at):
             image = more * x_ref[1, c, b, padded, :] - w0 * x_ref[2, c, b, padded, :]
             r = r_ref[c, b, at, :] - w1 * image
             q = second(l_ref[0, c, b, at, :], l_ref[1, c, b, at, :], l_ref[2, c, b, at, :])
             q = q + d_ref[c, b, at, :] * r
-            return sums[0] + r * r, sums[1] + r * q, sums[2] + r * image
-
-        gamma, delta, cross = over_tiles(dots2, (zero, zero, zero))
+            return r * r, r * q, r * image
+
+        gamma, delta, cross = sum_tiles(dots2, 3)
         delta = delta + energy(lambda at: second(gap_ref[0, at, :], gap_ref[1, at, :], gap_ref[2, at, :]))
         delta = delta - edges(lambda part: second(part(0), part(1), part(2)))
         start_sums(it + 2, gamma, delta, cross)
@@ -589,7 +600,7 @@
         finish(0, 0)
         apply_row(lu_ref, 0, 1, under)
         apply_strips(lu_ref, 0, left, right, range(1, groups))
-        lax.fori_loop(1, groups, finish, 0)
+        lax.fori_loop(1, groups, finish, 0, unroll=3)
 
         @pl.when(n < NEWTON - 1)
         def _():

time: 62.1 us -> 60 us (0.966)
  Pallas kernels: 59.8 us -> 57.7 us
    pallas_call x1, Pallas kernels: 59.8 us -> 57.7 us  [local(): pl.pallas_call(functools.partial(kernel, n_vol, n_zone), out_shape=[jax.S...]
where the time goes in v8:
time: 60 us; the launch traced here: 59.9 us
  Pallas kernels  57.7 us (96%)
  local copies, waits for them, and re-layouts  1.49 us (2%)
  between operations  0.64 us (1%)
    pallas_call x1, Pallas kernels, local(): pl.pallas_call(functools.partial(kernel, n_vol, n_zone), out_shape=[jax.S...  57.7 us
    unnamed x2, local copies, waits for them, and re-layouts  1.49 us

profile of v8, /device:TPU:1, one launch (start us, length us, event | category | flops | bytes accessed | tf_op | source)
XLA Modules:
  0.0 59.9 jit_solution(1971323145639878450)
XLA Ops:
  0.6 57.7 %shard_map.86 = (f32[3,128,256]{2,1,0:T(8,128)S(1)}, f32[3,128,256]{2,1,0:T(8,128)S(1)}) custom-call(f32[3,128,256]{2,1,0:T(8,128)} %load_hbm.1, f32[128,256]{1,0:T(8,128)} %stiff_hbm.1, s32[2,128]{1,0:T(2,128)} %bitcast.3, s32[1,1,16]{2,1,0:T(1,128)} %owner_hbm.1, s32[1,3,1,16]{3,2,1,0:T(1,128)} %bitcast.2, s32[1,1,16]{2,1,0:T(1,128)} %active_hbm.1, ...), custom_call_target="tpu_custom_call" | custom-call | tf_op jit(solution)/shard_map/pallas_call | solution.py:725
  58.4 0.7 %copy.11 = f32[3,128,256]{2,1,0:T(8,128)} copy(f32[3,128,256]{2,1,0:T(8,128)S(1)} %get-tuple-element.4) | data formatting | bytes 786432
  59.1 0.7 %copy.12 = f32[3,128,256]{2,1,0:T(8,128)} copy(f32[3,128,256]{2,1,0:T(8,128)S(1)} %get-tuple-element.5) | data formatting | bytes 786432

commit v9 on v8

--- a/solution.py
+++ b/solution.py
@@ -30,7 +30,7 @@
     u_ref, res_ref,
     load_ref, stiff_ref, flags_ref, owner_ref, pattern_ref, active_ref, mort_ref,
     x_ref, l_ref, r_ref, d_ref, lu_ref, hard_ref, contact_ref, halo_ref, own_ref, slot_ref, coef_ref, gap_ref, scale_ref,
-    mhi_ref, mlo_ref, spread_ref, push_ref,
+    mhl_ref, spread_ref, push_ref,
     surf_ref, block_ref, back_ref,
     pack_tab, unpack_tab,
     fsend, frecv0, frecv1, frecv2, fixed, bsend, brecv0, brecv1, brecv2, rsend, rrecv, csend, crecv, ssend, srecv,
@@ -119,8 +119,8 @@
         for k in range(NNZ):
             piece = mort_ref[r, k] if k == 0 else -mort_ref[r, k]
             high = piece.astype(BF16)
-            mhi_ref[r, :, k * BLK:(k + 1) * BLK] = high
-            mlo_ref[r, :, k * BLK:(k + 1) * BLK] = (piece - high.astype(F32)).astype(BF16)
+            mhl_ref[r, 0:BLK, k * BLK:(k + 1) * BLK] = high
+            mhl_ref[r, BLK:2 * BLK, k * BLK:(k + 1) * BLK] = (piece - high.astype(F32)).astype(BF16)
         return 0
 
     def set_up():
@@ -345,18 +345,16 @@
     def find_gaps(j):
         for r in range(rows):
             picked = split_rows(jnp.concatenate([slot_ref[j, link(r, k)] for k in range(NNZ)], axis=1))
-            gap = lax.dot_general(picked, mhi_ref[r], contract_last, preferred_element_type=F32)
-            gap = gap + lax.dot_general(picked, mlo_ref[r], contract_last, preferred_element_type=F32)
-            gap_ref[j, r * 8:r * 8 + 8, :] = join_rows(gap)
+            gap = lax.dot_general(picked, mhl_ref[r], contract_last, preferred_element_type=F32)
+            gap_ref[j, r * 8:r * 8 + 8, :] = join_rows(gap[:, 0:BLK] + gap[:, BLK:2 * BLK])
 
     def push_forces(j, n):
         it = n * KRY + j
         for r in range(rows):
             at = slice(r * 8, r * 8 + 8)
             multiplier = split_rows((scale_ref[at, :] * gap_ref[j, at, :])[0:4])
-            force = jnp.dot(multiplier, mhi_ref[r], preferred_element_type=F32)
-            force = force + jnp.dot(multiplier, mlo_ref[r], preferred_element_type=F32)
-            force = join_rows(force)
+            multiplier = jnp.concatenate([multiplier, multiplier], axis=1)
+            force = join_rows(jnp.dot(multiplier, mhl_ref[r], preferred_element_type=F32))
             high = force.astype(BF16).astype(F32)
             rest = force - high
             middle = rest.astype(BF16).astype(F32)
@@ -746,8 +744,7 @@
             pltpu.VMEM((KRY, 8, BLK), F32),
             pltpu.VMEM((KRY, rows * 8, BLK), F32),
             pltpu.VMEM((rows * 8, BLK), F32),
-            pltpu.VMEM((rows, BLK, NNZ * BLK), BF16),
-            pltpu.VMEM((rows, BLK, NNZ * BLK), BF16),
+            pltpu.VMEM((rows, 2 * BLK, NNZ * BLK), BF16),
             pltpu.VMEM((slots * 4, wide), BF16),
             pltpu.VMEM((wide, BLK), F32),
             pltpu.VMEM((blocks * 8, BLK), F32),

time: 60 us -> 59 us (0.983)
  Pallas kernels: 57.7 us -> 56.8 us
    pallas_call x1, Pallas kernels: 57.7 us -> 56.8 us  [local(): pl.pallas_call(functools.partial(kernel, n_vol, n_zone), out_shape=[jax.S...]
where the time goes in v9:
time: 59 us; the launch traced here: 58.9 us
  Pallas kernels  56.8 us (96%)
  local copies, waits for them, and re-layouts  1.49 us (3%)
  between operations  0.64 us (1%)
    pallas_call x1, Pallas kernels, local(): pl.pallas_call(functools.partial(kernel, n_vol, n_zone), out_shape=[jax.S...  56.8 us
    unnamed x2, local copies, waits for them, and re-layouts  1.49 us

profile of v9, /device:TPU:1, one launch (start us, length us, event | category | flops | bytes accessed | tf_op | source)
XLA Modules:
  0.0 58.9 jit_solution(6241878448118853113)
XLA Ops:
  0.6 56.8 %shard_map.86 = (f32[3,128,256]{2,1,0:T(8,128)S(1)}, f32[3,128,256]{2,1,0:T(8,128)S(1)}) custom-call(f32[3,128,256]{2,1,0:T(8,128)} %load_hbm.1, f32[128,256]{1,0:T(8,128)} %stiff_hbm.1, s32[2,128]{1,0:T(2,128)} %bitcast.3, s32[1,1,16]{2,1,0:T(1,128)} %owner_hbm.1, s32[1,3,1,16]{3,2,1,0:T(1,128)} %bitcast.2, s32[1,1,16]{2,1,0:T(1,128)} %active_hbm.1, ...), custom_call_target="tpu_custom_call" | custom-call | tf_op jit(solution)/shard_map/pallas_call | solution.py:723
  57.4 0.7 %copy.11 = f32[3,128,256]{2,1,0:T(8,128)} copy(f32[3,128,256]{2,1,0:T(8,128)S(1)} %get-tuple-element.4) | data formatting | bytes 786432
  58.2 0.7 %copy.12 = f32[3,128,256]{2,1,0:T(8,128)} copy(f32[3,128,256]{2,1,0:T(8,128)S(1)} %get-tuple-element.5) | data formatting | bytes 786432

commit v10 on v9

--- a/solution.py
+++ b/solution.py
@@ -505,7 +505,11 @@
         inner(2)
         fill_slots(2, n)
         find_gaps(2)
-        push_forces(2, n)
+
+        @pl.when(n < NEWTON - 1)
+        def _():
+            push_forces(2, 0)
+
         gamma1, delta, cross = finish_sums(it + 1)
         beta1 = gamma1 / gamma0
         pq1 = delta + beta1 * (2.0 * cross + beta1 * pq0)
@@ -528,6 +532,10 @@
         delta = delta + energy(lambda at: second(gap_ref[0, at, :], gap_ref[1, at, :], gap_ref[2, at, :]))
         delta = delta - edges(lambda part: second(part(0), part(1), part(2)))
         start_sums(it + 2, gamma, delta, cross)
+
+        @pl.when(n == NEWTON - 1)
+        def _():
+            push_forces(2, NEWTON - 1)
 
         @pl.when(n < NEWTON - 1)
         def _():

time: 59 us -> 59 us (level)
  no operation moved by 1% of the time
where the time goes in v10:
time: 59 us; the launch traced here: 58.9 us
  Pallas kernels  56.8 us (96%)
  local copies, waits for them, and re-layouts  1.49 us (3%)
  between operations  0.64 us (1%)
    pallas_call x1, Pallas kernels, local(): pl.pallas_call(functools.partial(kernel, n_vol, n_zone), out_shape=[jax.S...  56.8 us
    unnamed x2, local copies, waits for them, and re-layouts  1.49 us

profile of v10, /device:TPU:1, one launch (start us, length us, event | category | flops | bytes accessed | tf_op | source)
XLA Modules:
  0.0 58.9 jit_solution(17678324935038455718)
XLA Ops:
  0.6 56.8 %shard_map.86 = (f32[3,128,256]{2,1,0:T(8,128)S(1)}, f32[3,128,256]{2,1,0:T(8,128)S(1)}) custom-call(f32[3,128,256]{2,1,0:T(8,128)} %load_hbm.1, f32[128,256]{1,0:T(8,128)} %stiff_hbm.1, s32[2,128]{1,0:T(2,128)} %bitcast.3, s32[1,1,16]{2,1,0:T(1,128)} %owner_hbm.1, s32[1,3,1,16]{3,2,1,0:T(1,128)} %bitcast.2, s32[1,1,16]{2,1,0:T(1,128)} %active_hbm.1, ...), custom_call_target="tpu_custom_call" | custom-call | tf_op jit(solution)/shard_map/pallas_call | solution.py:731
  57.4 0.7 %copy.11 = f32[3,128,256]{2,1,0:T(8,128)} copy(f32[3,128,256]{2,1,0:T(8,128)S(1)} %get-tuple-element.4) | data formatting | bytes 786432
  58.2 0.7 %copy.12 = f32[3,128,256]{2,1,0:T(8,128)} copy(f32[3,128,256]{2,1,0:T(8,128)S(1)} %get-tuple-element.5) | data formatting | bytes 786432
